TPU v7x, 32 devices: a whole 2x2x4 slice. The times are simulated.
32 devices in a mesh: ens: 4 (over y, x), space: 8 (over z, core).
Axes of the slice: x: 2, y: 2, z: 4, core: 2. Of those that a mesh axis runs over, the one named last changes fastest.
Arguments:
- inputs: bfloat16 [8, 32, 256, 256], P('ens', None, 'space'), may hold values from -6 to 6
- target: bfloat16 [32, 256, 256], P(None, 'space'), may hold values from -6 to 6
- filter_taps: bfloat16 [3, 32, 3, 9], replicated, may hold values from -1.75 to 1.75
- lon_offset: int32 [32], replicated, may hold values from -2 to 2, as said below
- lon_width: int32 [32], replicated, may hold values from 1 to 4
- w_disco: bfloat16 [3, 256, 256], replicated, may hold values from -0.21875 to 0.21875
- w_up: bfloat16 [256, 512], replicated, may hold values from -0.375 to 0.375
- w_down: bfloat16 [512, 256], replicated, may hold values from -0.25 to 0.25
- norm_gain: float32 [256], replicated, may hold values from 0.5 to 1.5
Outputs:
- grad_input: bfloat16 [8, 32, 256, 256], P('ens', None, 'space')
- grad_disco: float32 [3, 256, 256], replicated
- grad_up: float32 [256, 512], replicated
- grad_down: float32 [512, 256], replicated
- grad_gain: float32 [256], replicated
Inputs may be any that keep to these rules, and one draw needn't show every extreme that they name: |lon_offset| + lon_width <= 4 in every row; some row has offset 0 and width 4, some row offset 2, some row offset -2.
All inputs are finite; a program needn't handle non-finite values.
Results may differ from a plain program's by a relative error of at most 0.02.
Values may be sent and summed in bfloat16 or wider, within the bound.
A program may use at most 128 MiB of HBM per device.

v0:
```python
import math

import jax
import jax.numpy as jnp
from jax import lax
from jax.sharding import PartitionSpec as P

root_two_pi = 0.7978845608028654


def padded_2(block, sides, width):
    for axis, dim in sides:
        count = lax.axis_size(axis)
        forward = [(i, i + 1) for i in range(count - 1)]
        forward.append((count - 1, 0))
        backward = [(target, source) for source, target in forward]
        low = lax.ppermute(
            lax.slice_in_dim(block, block.shape[dim] - width, None, axis=dim), axis, forward
        )
        high = lax.ppermute(lax.slice_in_dim(block, 0, width, axis=dim), axis, backward)
        block = jnp.concatenate([low, block, high], axis=dim)
    return block


def slope_abs(values):
    return values * lax.rsqrt(values * values + 0.01)


def gelu_value(preact):
    return (
        0.5
        * preact
        * (1.0 + jnp.tanh(root_two_pi * (preact + 0.044715 * preact * preact * preact)))
    )


def gelu_slope(preact):
    tangent = jnp.tanh(root_two_pi * (preact + 0.044715 * preact * preact * preact))
    return 0.5 * (1.0 + tangent) + 0.5 * preact * (1.0 - tangent * tangent) * root_two_pi * (
        1.0 + 3.0 * 0.044715 * preact * preact
    )


def masked_taps(filter_taps, lon_offset, lon_width):
    count = filter_taps.shape[3]
    reach = (count - 1) // 2
    offsets = jnp.arange(count, dtype=jnp.int32) - reach
    keep = jnp.abs(offsets[None, :] - lon_offset[:, None]) <= lon_width[:, None]
    return jnp.where(keep[None, :, None, :], filter_taps, jnp.zeros_like(filter_taps))


def band_matrix(taps, local, mirror):
    count = taps.shape[3]
    reach = (count - 1) // 2
    across = jnp.arange(local + 2 * reach, dtype=jnp.int32)[None, :]
    along = jnp.arange(local, dtype=jnp.int32)[:, None]
    if mirror:
        offset = 2 * reach + along - across
    else:
        offset = across - along
    inside = (offset >= 0) & (offset < count)
    picked = jnp.take(taps, jnp.clip(offset, 0, count - 1), axis=3)
    return jnp.where(inside, picked, jnp.zeros_like(picked))


def crps_slope(owned, everyone, aimed):
    mine = owned.astype(jnp.float32)
    miss = slope_abs(mine - aimed.astype(jnp.float32))
    spread = jnp.sum(slope_abs(mine[:, None] - everyone.astype(jnp.float32)[None]), axis=1)
    return (miss - spread / (everyone.shape[0] - 1)).astype(jnp.bfloat16)


def body(inputs, target, filter_taps, lon_offset, lon_width, w_disco, w_up, w_down, norm_gain):
    taps = masked_taps(filter_taps, lon_offset, lon_width)
    reach = (taps.shape[3] - 1) // 2
    members_here = inputs.shape[0]
    rows = inputs.shape[1]
    local = inputs.shape[2]
    channels = inputs.shape[3]
    ahead = band_matrix(taps, local, False)
    padded_lon = padded_2(inputs, (("space", 2),), reach)
    padded = jnp.pad(padded_lon, ((0, 0), (1, 1), (0, 0), (0, 0)))
    total = jnp.zeros((taps.shape[0],) + inputs.shape, jnp.float32)
    for shift_row in range(3):
        total = total + jnp.einsum(
            "kijp,mipc->kmijc",
            ahead[:, :, shift_row],
            padded[:, shift_row : shift_row + rows],
            preferred_element_type=jnp.float32,
        )
    filtered = total.astype(jnp.bfloat16)
    hidden = jnp.einsum("kmijc,kcd->mijd", filtered, w_disco, preferred_element_type=jnp.float32)
    inverse = lax.rsqrt(jnp.mean(hidden * hidden, axis=-1, keepdims=True) + 1e-06)
    scaled = hidden * inverse
    normed = (scaled * norm_gain).astype(jnp.bfloat16)
    preact = jnp.einsum("mijc,cf->mijf", normed, w_up, preferred_element_type=jnp.float32)
    active = gelu_value(preact).astype(jnp.bfloat16)
    output = (
        inputs.astype(jnp.float32)
        + jnp.einsum("mijf,fc->mijc", active, w_down, preferred_element_type=jnp.float32)
    ).astype(jnp.bfloat16)
    everyone = lax.all_gather(output, "ens", axis=0, tiled=True)
    dgrad = crps_slope(output, everyone, target[None])
    down_part = jnp.einsum("mijf,mijc->fc", active, dgrad, preferred_element_type=jnp.float32)
    dactive = jnp.einsum("mijc,fc->mijf", dgrad, w_down, preferred_element_type=jnp.float32).astype(
        jnp.bfloat16
    )
    dpre = (dactive.astype(jnp.float32) * gelu_slope(preact)).astype(jnp.bfloat16)
    up_part = jnp.einsum("mijc,mijf->cf", normed, dpre, preferred_element_type=jnp.float32)
    dnorm = jnp.einsum("mijf,cf->mijc", dpre, w_up, preferred_element_type=jnp.float32)
    gain_part = jnp.sum(dnorm * scaled, axis=(0, 1, 2))
    dscaled = dnorm * norm_gain
    dhidden = (
        inverse * (dscaled - scaled * jnp.mean(dscaled * scaled, axis=-1, keepdims=True))
    ).astype(jnp.bfloat16)
    disco_part = jnp.einsum(
        "kmijc,mijd->kcd", filtered, dhidden, preferred_element_type=jnp.float32
    )
    dfilt = jnp.einsum(
        "mijd,kcd->kmijc", dhidden, w_disco, preferred_element_type=jnp.float32
    ).astype(jnp.bfloat16)
    mirrored = band_matrix(taps, local, True)
    beside_all = padded_2(dfilt, (("space", 3),), reach)
    placed = jnp.zeros((members_here, rows + 2, local, channels), jnp.float32)
    for shift_row in range(3):
        placed = placed.at[:, shift_row : shift_row + rows].add(
            jnp.einsum(
                "kijp,kmipc->mijc",
                mirrored[:, :, shift_row],
                beside_all,
                preferred_element_type=jnp.float32,
            )
        )
    spread_back = placed[:, 1 : rows + 1]
    grad_input = (dgrad.astype(jnp.float32) + spread_back).astype(jnp.bfloat16)
    sums = lax.psum((disco_part, up_part, down_part, gain_part), ("ens", "space"))
    factor = 1.0 / math.sqrt(
        members_here * lax.axis_size("ens") * rows * local * lax.axis_size("space")
    )
    return (grad_input, sums[0] * factor, sums[1] * factor, sums[2] * factor, sums[3] * factor)


def solution(mesh):
    placed = (
        P("ens", None, "space", None),
        P(None, "space", None),
        P(),
        P(),
        P(),
        P(),
        P(),
        P(),
        P(),
    )
    return jax.shard_map(
        body,
        mesh=mesh,
        in_specs=placed,
        out_specs=(P("ens", None, "space", None), P(), P(), P(), P()),
        check_vma=False,
    )
```

profile of v0, /device:TPU:0, one launch (start us, length us, event | category | flops | bytes accessed | tf_op | source)
XLA Modules:
  0.0 265.7 jit_solution(9336772968789892579)
XLA Ops:
  7.2 1.2 fusion.57
  8.9 4.1 %collective-permute-start.1 = (bf16[2,32,4,256]{3,2,0,1:T(4,128)(2,1)S(1)}, bf16[2,32,4,256]{3,2,0,1:T(4,128)(2,1)S(1)}, u32[]{:S(2)}, u32[]{:S(2)}) collective-permute-start(bf16[2,32,4,256]{3,2,0,1:T(4,128)(2,1)S(1)} %get-tuple-element.50), channel_id=1, source_target_pairs={{1,0},{2,1},{3,2},{4,3},{5,4},{6,5},{7,6},{0,7},{9,8},{10,9},{11,1... | collective-permute-start | bytes 393224 | tf_op jit(solution)/shard_map/ppermute | solution.py:20
  14.7 7.2 %gather_fusion = bf16[1280,3,32,3]{2,3,1,0:T(4,128)(2,1)} fusion(bf16[3,32,3,9]{1,2,3,0:T(4,128)(2,1)S(1)} %broadcast_select_fusion, s32[2048]{0:T(1024)S(1)} %pad_clamp_fusion.1), kind=kCustom, calls=%fused_computation.clone | custom fusion | bytes 1479680 | tf_op jit(solution)/shard_map/jit(_take)/gather | solution.py:62
  21.9 7.8 %copy.69 = bf16[32,40,3,32,3]{1,0,2,3,4:T(8,128)(2,1)S(1)} copy(bf16[32,40,3,32,3]{3,4,2,1,0:T(4,128)(2,1)} %bitcast.147) | data formatting | bytes 1474560 | tf_op jit(solution)/shard_map/jit(_take)/gather | solution.py:62
  33.6 1.3 fusion.10
  35.0 1.1 fusion.16
  36.7 3.3 %multiply_convert_fusion = (bf16[2,32,32,512]{3,2,1,0:T(8,128)(2,1)S(1)}, f32[2,32,32,512]{3,2,1,0:T(8,128)}) fusion(bf16[256,512]{1,0:T(8,128)(2,1)S(1)} %copy-done.17, f32[2,32,32,256,1]{3,2,4,1,0:T(8,128)S(1)} %get-tuple-element.54, f32[256]{0:T(256)S(1)} %copy-done.18, f32[2,32,32]{2,1,0:T(8,128)S(1)} %add_rsqrt_fusion), kind=kOutput, calls=%fused_computation.17 | convolution fusion | flops 547880960 | bytes 8659968 | tf_op jit(solution)/shard_map/mijc,cf->mijf/dot_general | solution.py:96
  39.9 2.4 fusion.58
  42.6 1.1 convert_element_type.64
  43.9 7.3 %gather_fusion.1 = bf16[1280,3,32,3]{2,3,1,0:T(4,128)(2,1)} fusion(bf16[3,32,3,9]{1,2,3,0:T(4,128)(2,1)S(1)} %broadcast_select_fusion, s32[2048]{0:T(1024)S(1)} %pad_clamp_fusion), kind=kCustom, calls=%fused_computation.1.clone | custom fusion | bytes 1479680 | tf_op jit(solution)/shard_map/jit(_take)/gather | solution.py:62
  51.2 7.8 %copy.72 = bf16[32,40,3,32,3]{1,0,2,3,4:T(8,128)(2,1)S(1)} copy(bf16[32,40,3,32,3]{3,4,2,1,0:T(4,128)(2,1)} %bitcast.146) | data formatting | bytes 1474560 | tf_op jit(solution)/shard_map/jit(_take)/gather | solution.py:62
  59.1 1.8 bitcast_select_fusion
  60.9 34.3 %all-gather.2.cloned.1.call-done = bf16[8,32,32,256]{3,2,1,0:T(8,128)(2,1)} async-done(((bf16[2,32,32,256]{3,2,1,0:T(8,128)(2,1)}), bf16[8,32,32,256]{3,2,1,0:T(8,128)(2,1)}) %all-gather.2.cloned.1.call-update) | async-done | bytes 4194320 | tf_op jit(solution)/shard_map/all_gather | solution.py:102
  95.1 3.2 %convert_element_type.65 = f32[8,32,32,256]{3,2,1,0:T(8,128)S(1)} convert(bf16[8,32,32,256]{3,2,1,0:T(8,128)(2,1)} %all-gather.2.cloned.1.call-done) | non-fusion elementwise | flops 2097152 | bytes 12582912 | tf_op jit(solution)/shard_map/convert_element_type | solution.py:69
  98.4 3.5 %fusion.2 = f32[2,32,32,256]{3,2,1,0:T(8,128)S(1)} fusion(f32[8,32,32,256]{3,2,1,0:T(8,128)S(1)} %convert_element_type.65, f32[2,32,32,256]{3,2,1,0:T(8,128)S(1)} %copy-done.3), kind=kLoop, calls=%fused_computation.6 | loop fusion | flops 20447232 | bytes 12582912 | tf_op jit(solution)/shard_map/reduce_sum | solution.py:69
  102.7 1.9 copy-done.19
  104.6 2.9 %fusion.9 = bf16[2,32,32,512]{3,2,1,0:T(8,128)(2,1)S(1)} fusion(f32[2,32,32,512]{3,2,1,0:T(8,128)S(1)} %copy-done.19, bf16[2,32,32,256]{3,2,1,0:T(8,128)(2,1)S(1)} %subtract_convert_fusion, bf16[512,256]{1,0:T(8,128)(2,1)S(1)} %copy-done.16), kind=kOutput, calls=%fused_computation.16 | convolution fusion | flops 558891008 | bytes 7602176 | tf_op jit(solution)/shard_map/mijc,fc->mijf/dot_general | solution.py:105
  107.5 2.2 fusion.30
  111.5 1.1 copy-done.10
  112.6 1.9 convolution_bitcast_fusion.1
  115.6 1.2 fusion.56
  116.8 3.5 %collective-permute-start.3 = (bf16[3,2,32,4,256]{4,3,0,2,1:T(4,128)(2,1)}, bf16[3,2,32,4,256]{4,3,0,2,1:T(4,128)(2,1)}, u32[]{:S(2)}, u32[]{:S(2)}) collective-permute-start(bf16[3,2,32,4,256]{4,3,0,2,1:T(4,128)(2,1)} %get-tuple-element.48), channel_id=1, source_target_pairs={{1,0},{2,1},{3,2},{4,3},{5,4},{6,5},{7,6},{0,7},{9,8},{10,9},{11,1... | collective-permute-start | bytes 1179656 | tf_op jit(solution)/shard_map/ppermute | solution.py:20
  120.4 1.5 fusion.33
  121.9 38.0 %psum.31 = f32[256]{0:T(256)S(1)} all-reduce(f32[256]{0:T(256)S(1)} %get-tuple-element.42), channel_id=1, replica_groups=mesh['ens'=4,'space'=8] {'ens','space'}, use_global_device_ids=true, to_apply=%region_7.9 | all-reduce | flops 256 | bytes 2048 | tf_op jit(solution)/shard_map/psum | solution.py:136
  160.5 2.9 %convolution_bitcast_fusion = f32[2,32,32,256]{3,2,1,0:T(8,128)S(1)} fusion(bf16[3,32,3,32,40]{4,3,0,1,2:T(8,128)(2,1)} %bitcast_select_fusion, bf16[3,2,32,4,256]{4,3,0,2,1:T(4,128)(2,1)} %collective-permute-done.3, bf16[3,2,32,32,256]{4,3,0,2,1:T(8,128)(2,1)S(1)} %convert_bitcast_fusion, bf16[3,2,32,4,256]{4,3,0,2,1:T(4,128)(2,1)} %collective-permute-done.2), kind=kOutput, calls=%fused_computation.44 | convolution fusion | flops 137625600 | bytes 6815744 | tf_op jit(solution)/shard_map/kijp,kmipc->mijc/dot_general | solution.py:127
  163.6 1.5 copy-done.11
  165.1 3.1 %fusion.15 = f32[2,34,32,256]{3,2,1,0:T(8,128)S(1)} fusion(f32[2,34,32,256]{3,2,1,0:T(8,128)S(1)} %scatter-add.10, bf16[3,32,3,32,40]{4,3,0,1,2:T(8,128)(2,1)S(1)} %copy-done.11, bf16[3,2,32,4,256]{4,3,0,2,1:T(4,128)(2,1)} %collective-permute-done.3, bf16[3,2,32,32,256]{4,3,0,2,1:T(8,128)(2,1)S(1)} %convert_bitcast_fusion, ...), kind=kOutput, calls=%fused_computation.30 | convolution fusion | flops 138149888 | bytes 8912896 | tf_op jit(solution)/shard_map/kijp,kmipc->mijc/dot_general | solution.py:127
  168.2 3.2 %fusion.14 = f32[2,34,32,256]{3,2,1,0:T(8,128)S(1)} fusion(f32[2,34,32,256]{3,2,1,0:T(8,128)S(1)} %fusion.15, bf16[3,32,3,32,40]{4,3,0,1,2:T(8,128)(2,1)S(1)} %copy-done.11, bf16[3,2,32,4,256]{4,3,0,2,1:T(4,128)(2,1)} %collective-permute-done.3, bf16[3,2,32,32,256]{4,3,0,2,1:T(8,128)(2,1)S(1)} %convert_bitcast_fusion, ...), kind=kOutput, calls=%fused_computation.28 | convolution fusion | flops 138149888 | bytes 8912896 | tf_op jit(solution)/shard_map/kijp,kmipc->mijc/dot_general | solution.py:127
  171.3 1.4 fusion.13
  172.7 81.3 %all-reduce.5.cloned.1.call-done = (f32[3,256,256]{2,1,0:T(8,128)}, f32[256,512]{1,0:T(8,128)}, f32[512,256]{1,0:T(8,128)}) async-done(((f32[3,256,256]{2,1,0:T(8,128)}, f32[256,512]{1,0:T(8,128)}, f32[512,256]{1,0:T(8,128)}), (f32[3,256,256]{2,1,0:T(8,128)}, f32[256,512]{1,0:T(8,128)}, f32[512,256]{1,0:T(8,128)})) %all-reduce.5.cloned.1.call-update) | async-done | bytes 1835024 | tf_op jit(solution)/shard_map/psum | solution.py:136
  254.1 2.1 broadcast_multiply_fusion
  256.2 1.9 broadcast_multiply_fusion.1
  (72 shorter events, 12.2 us)
Async XLA Ops:
  7.2 27.8 %copy-start = (bf16[3,256,256]{2,1,0:T(8,128)(2,1)S(1)}, bf16[3,256,256]{2,1,0:T(8,128)(2,1)}, u32[]{:S(2)}) copy-start(bf16[3,256,256]{2,1,0:T(8,128)(2,1)} %param.22) | copy-start | bytes 1179652
  7.2 88.0 %all-gather.2.cloned.1.call-start = ((), (), s32[]{:S(2)}) async-start(), calls=%async_computation | async-start | bytes 5242880 | tf_op jit(solution)/shard_map/all_gather | solution.py:102
  8.4 21.5 %collective-permute-start = (bf16[2,32,4,256]{3,2,0,1:T(4,128)(2,1)S(1)}, bf16[2,32,4,256]{3,2,0,1:T(4,128)(2,1)S(1)}, u32[]{:S(2)}, u32[]{:S(2)}) collective-permute-start(bf16[2,32,4,256]{3,2,0,1:T(4,128)(2,1)S(1)} %get-tuple-element.49), channel_id=1, source_target_pairs={{0,1},{1,2},{2,3},{3,4},{4,5},{5,6},{6,7},{7,0},{8,9},{9,10},{10,1... | collective-permute-start | bytes 393224 | tf_op jit(solution)/shard_map/ppermute | solution.py:17
  8.9 21.0 %collective-permute-start.1 = (bf16[2,32,4,256]{3,2,0,1:T(4,128)(2,1)S(1)}, bf16[2,32,4,256]{3,2,0,1:T(4,128)(2,1)S(1)}, u32[]{:S(2)}, u32[]{:S(2)}) collective-permute-start(bf16[2,32,4,256]{3,2,0,1:T(4,128)(2,1)S(1)} %get-tuple-element.50), channel_id=1, source_target_pairs={{1,0},{2,1},{3,2},{4,3},{5,4},{6,5},{7,6},{0,7},{9,8},{10,9},{11,1... | collective-permute-start | bytes 393224 | tf_op jit(solution)/shard_map/ppermute | solution.py:20
  29.7 1.2 copy-start.1
  35.0 1.6 copy-start.9
  35.0 1.7 copy-start.17
  35.0 1.7 copy-start.18
  36.6 3.3 %copy-start.4 = (f32[2,32,32,256,1]{3,2,4,1,0:T(8,128)}, f32[2,32,32,256,1]{3,2,4,1,0:T(8,128)S(1)}, u32[]{:S(2)}) copy-start(f32[2,32,32,256,1]{3,2,4,1,0:T(8,128)S(1)} %get-tuple-element.54) | copy-start | bytes 6291460
  36.6 3.3 %copy-start.16 = (bf16[512,256]{1,0:T(8,128)(2,1)S(1)}, bf16[512,256]{1,0:T(8,128)(2,1)}, u32[]{:S(2)}) copy-start(bf16[512,256]{1,0:T(8,128)(2,1)} %param.24) | copy-start | bytes 786436
  39.9 2.4 copy-start.12
  39.9 2.7 %copy-start.14 = (bf16[32,32,256]{2,1,0:T(8,128)(2,1)S(1)}, bf16[32,32,256]{2,1,0:T(8,128)(2,1)}, u32[]{:S(2)}) copy-start(bf16[32,32,256]{2,1,0:T(8,128)(2,1)} %param.18) | copy-start | bytes 1572868
  42.4 211.7 %all-reduce.5.cloned.1.call-start = ((), (), s32[]{:S(2)}) async-start(), calls=%async_computation.1 | async-start | bytes 3670016 | tf_op jit(solution)/shard_map/psum | solution.py:136
  60.8 37.5 %copy-start.3 = (f32[2,32,32,256]{3,2,1,0:T(8,128)S(1)}, f32[2,32,32,256]{3,2,1,0:T(8,128)}, u32[]{:S(2)}) copy-start(f32[2,32,32,256]{3,2,1,0:T(8,128)} %get-tuple-element.57) | copy-start | bytes 6291460
  98.4 3.6 %copy-start.2 = (bf16[2,32,32,256]{3,2,1,0:T(8,128)(2,1)S(1)}, bf16[2,32,32,256]{3,2,1,0:T(8,128)(2,1)}, u32[]{:S(2)}) copy-start(bf16[2,32,32,256]{3,2,1,0:T(8,128)(2,1)} %get-tuple-element.58) | copy-start | bytes 3145732
  98.4 3.6 %copy-start.6 = (f32[32,32,256]{2,1,0:T(8,128)S(1)}, f32[32,32,256]{2,1,0:T(8,128)}, u32[]{:S(2)}) copy-start(f32[32,32,256]{2,1,0:T(8,128)} %convert_element_type.64) | copy-start | bytes 3145732
  102.0 2.6 copy-start.19
  102.6 17.7 %copy-start.7 = (bf16[2,32,32,256]{3,2,1,0:T(8,128)(2,1)}, bf16[2,32,32,256]{3,2,1,0:T(8,128)(2,1)S(1)}, u32[]{:S(2)}) copy-start(bf16[2,32,32,256]{3,2,1,0:T(8,128)(2,1)S(1)} %subtract_convert_fusion) | copy-start | bytes 3145732
  104.6 3.0 %copy-start.5 = (f32[2,32,32,256,1]{3,2,4,1,0:T(8,128)S(1)}, f32[2,32,32,256,1]{3,2,4,1,0:T(8,128)}, u32[]{:S(2)}) copy-start(f32[2,32,32,256,1]{3,2,4,1,0:T(8,128)} %copy-done.4) | copy-start | bytes 6291460
  110.7 1.9 copy-start.10
  114.5 5.8 %copy-start.13 = (bf16[2,32,32,512]{3,2,1,0:T(8,128)(2,1)S(1)}, bf16[2,32,32,512]{3,2,1,0:T(8,128)(2,1)}, u32[]{:S(2)}) copy-start(bf16[2,32,32,512]{3,2,1,0:T(8,128)(2,1)} %copy-done.12) | copy-start | bytes 6291460
  116.8 43.7 %collective-permute-start.2 = (bf16[3,2,32,4,256]{4,3,0,2,1:T(4,128)(2,1)}, bf16[3,2,32,4,256]{4,3,0,2,1:T(4,128)(2,1)}, u32[]{:S(2)}, u32[]{:S(2)}) collective-permute-start(bf16[3,2,32,4,256]{4,3,0,2,1:T(4,128)(2,1)} %get-tuple-element.47), channel_id=1, source_target_pairs={{0,1},{1,2},{2,3},{3,4},{4,5},{5,6},{6,7},{7,0},{8,9},{9,10},{10,1... | collective-permute-start | bytes 1179656 | tf_op jit(solution)/shard_map/ppermute | solution.py:17
  116.8 43.7 %collective-permute-start.3 = (bf16[3,2,32,4,256]{4,3,0,2,1:T(4,128)(2,1)}, bf16[3,2,32,4,256]{4,3,0,2,1:T(4,128)(2,1)}, u32[]{:S(2)}, u32[]{:S(2)}) collective-permute-start(bf16[3,2,32,4,256]{4,3,0,2,1:T(4,128)(2,1)} %get-tuple-element.48), channel_id=1, source_target_pairs={{1,0},{2,1},{3,2},{4,3},{5,4},{6,5},{7,6},{0,7},{9,8},{10,9},{11,1... | collective-permute-start | bytes 1179656 | tf_op jit(solution)/shard_map/ppermute | solution.py:20
  163.4 1.7 copy-start.11
  168.2 3.2 %copy-start.8 = (bf16[2,32,32,256]{3,2,1,0:T(8,128)(2,1)S(1)}, bf16[2,32,32,256]{3,2,1,0:T(8,128)(2,1)}, u32[]{:S(2)}) copy-start(bf16[2,32,32,256]{3,2,1,0:T(8,128)(2,1)} %copy-done.7) | copy-start | bytes 3145732
  254.1 4.0 %copy-start.15 = (f32[256,512]{1,0:T(8,128)S(1)}, f32[256,512]{1,0:T(8,128)}, u32[]{:S(2)}) copy-start(f32[256,512]{1,0:T(8,128)} %get-tuple-element.45) | copy-start | bytes 1572868
Sparse Core Ops, SparseCore 0:
  42.5 52.6 all-gather.1
  122.0 131.9 all-reduce.4
where the time goes:
time: 267 us; the launch traced here: 266 us
  waiting for transfers between devices  116 us (43%)
  local copies, waits for them, and re-layouts  38.9 us (15%)
  blocking collectives  38 us (14%)
  matrix products  29.7 us (11%)
  other arithmetic  20.7 us (8%)
  between operations  14.4 us (5%)
  starting transfers between devices  8.41 us (3%)
    psum x1, waiting for transfers between devices, body(): lax.psum((disco_part, up_part, down_part, gain_part), ('ens', 'space'))  81.3 us
    psum x1, blocking collectives, body(): lax.psum((disco_part, up_part, down_part, gain_part), ('ens', 'space'))  38 us
    all_gather x1, waiting for transfers between devices, body(): everyone = lax.all_gather(output, 'ens', axis=0, tiled=True)  34.3 us
    gather x4, local copies, waits for them, and re-layouts, band_matrix(): picked = jnp.take(taps, jnp.clip(offset, 0, count - 1), axis=3)  30.1 us
    dot_general x3, matrix products, body(): jnp.einsum('kijp,kmipc->mijc', mirrored[:, :, shift_row], beside_all, pre...  9.11 us
    ppermute x2, starting transfers between devices, padded_2(): lax.ppermute(lax.slice_in_dim(block, 0, width, axis=dim), axis, backward)  7.64 us
    unnamed x40, local copies, waits for them, and re-layouts  6.01 us
  transfers between devices with their start and end apart: 6, of which 2 were waited for; matrix products, arithmetic and copies ran while one was open for 18% of the time, Pallas kernels for 0%

commit v1 on v0

--- a/solution.py
+++ b/solution.py
@@ -1,10 +1,14 @@
+import functools
 import math
 
 import jax
 import jax.numpy as jnp
 from jax import lax
+from jax.experimental import pallas as pl
+from jax.experimental.pallas import tpu as pltpu
 from jax.sharding import PartitionSpec as P
 
+MESH = pl.DeviceIdType.MESH
 root_two_pi = 0.7978845608028654
 
 
@@ -58,9 +62,131 @@
         offset = 2 * reach + along - across
     else:
         offset = across - along
-    inside = (offset >= 0) & (offset < count)
-    picked = jnp.take(taps, jnp.clip(offset, 0, count - 1), axis=3)
-    return jnp.where(inside, picked, jnp.zeros_like(picked))
+    band = jnp.zeros(taps.shape[:3] + offset.shape, taps.dtype)
+    for step in range(count):
+        band = jnp.where(offset == step, taps[:, :, :, step, None, None], band)
+    return band
+
+
+def sum_kernel(members, halves, part_ref, full_ref, sum_core, sum_ens, from_core, from_ens, from_space, send, recv):
+    ens, space = lax.axis_index("ens"), lax.axis_index("space")
+    core, half = lax.rem(space, 2), space // 2
+    other = space + 1 - 2 * core
+    ens_peers = [(lax.rem(ens + d, members), space) for d in range(1, members)]
+    space_peers = [(ens, lax.rem(half + d, halves) * 2 + core) for d in range(1, halves)]
+    barrier = pltpu.get_barrier_semaphore()
+    everyone = [(ens, other)] + ens_peers + space_peers
+    for peer in everyone:
+        pl.semaphore_signal(barrier, inc=1, device_id=peer, device_id_type=MESH)
+    pl.semaphore_wait(barrier, len(everyone))
+
+    def move(src, dst, slot, peer):
+        copy = pltpu.make_async_remote_copy(
+            src_ref=src,
+            dst_ref=dst,
+            send_sem=send.at[slot],
+            recv_sem=recv.at[slot],
+            device_id=peer,
+            device_id_type=MESH,
+        )
+        copy.start()
+        return copy
+
+    wide = members * halves
+    first_core = core * wide
+    copies = [move(part_ref.at[pl.ds((1 - core) * wide, wide)], from_core, 0, (ens, other))]
+    for copy in copies:
+        copy.wait()
+
+    def add_core(i, carry):
+        total = part_ref[first_core + i].astype(jnp.float32) + from_core[i].astype(jnp.float32)
+        sum_core[i] = total.astype(jnp.bfloat16)
+        return carry
+
+    lax.fori_loop(0, wide, add_core, 0)
+
+    copies = []
+    for d in range(1, members):
+        peer = ens_peers[d - 1]
+        copies.append(move(sum_core.at[pl.ds(peer[0] * halves, halves)], from_ens.at[d - 1], d, peer))
+    for copy in copies:
+        copy.wait()
+
+    def add_ens(i, carry):
+        total = sum_core[ens * halves + i].astype(jnp.float32)
+        for d in range(members - 1):
+            total = total + from_ens[d, i].astype(jnp.float32)
+        sum_ens[i] = total.astype(jnp.bfloat16)
+        return carry
+
+    lax.fori_loop(0, halves, add_ens, 0)
+
+    copies = []
+    for d in range(1, halves):
+        copies.append(
+            move(sum_ens.at[lax.rem(half + d, halves)], from_space.at[d - 1], members - 1 + d, space_peers[d - 1])
+        )
+    for copy in copies:
+        copy.wait()
+    total = sum_ens[half].astype(jnp.float32)
+    for d in range(halves - 1):
+        total = total + from_space[d].astype(jnp.float32)
+    first_ens = first_core + ens * halves
+    full_ref[first_ens + half] = total.astype(jnp.bfloat16)
+
+    back = members + halves - 1
+    copies = []
+    for d in range(1, halves):
+        block = full_ref.at[pl.ds(first_ens + half, 1)]
+        copies.append(move(block, block, back + members - 1 + d, space_peers[d - 1]))
+    for copy in copies:
+        copy.wait()
+    copies = []
+    for d in range(1, members):
+        block = full_ref.at[pl.ds(first_ens, halves)]
+        copies.append(move(block, block, back + d, ens_peers[d - 1]))
+    for copy in copies:
+        copy.wait()
+    block = full_ref.at[pl.ds(first_core, wide)]
+    move(block, block, back, (ens, other)).wait()
+
+
+def sum_everywhere(parts):
+    members, halves = lax.axis_size("ens"), lax.axis_size("space") // 2
+    blocks = 2 * members * halves
+    width = parts[0].shape[1]
+    rows = sum(part.shape[0] for part in parts)
+    each = -(-rows // (blocks * 16)) * 16
+    packed = jnp.concatenate(
+        [part.astype(jnp.bfloat16) for part in parts]
+        + [jnp.zeros((blocks * each - rows, width), jnp.bfloat16)]
+    ).reshape(blocks, each, width)
+    whole = pl.BlockSpec(memory_space=pltpu.VMEM)
+    count = 2 * (members + halves - 1)
+    summed = pl.pallas_call(
+        functools.partial(sum_kernel, members, halves),
+        out_shape=jax.ShapeDtypeStruct(packed.shape, jnp.bfloat16),
+        in_specs=[whole],
+        out_specs=whole,
+        scratch_shapes=[
+            pltpu.VMEM((members * halves, each, width), jnp.bfloat16),
+            pltpu.VMEM((halves, each, width), jnp.bfloat16),
+            pltpu.VMEM((members * halves, each, width), jnp.bfloat16),
+            pltpu.VMEM((max(members - 1, 1), halves, each, width), jnp.bfloat16),
+            pltpu.VMEM((max(halves - 1, 1), each, width), jnp.bfloat16),
+            pltpu.SemaphoreType.DMA((count,)),
+            pltpu.SemaphoreType.DMA((count,)),
+        ],
+        compiler_params=pltpu.CompilerParams(
+            collective_id=1, has_side_effects=True, vmem_limit_bytes=24 * 1024 * 1024
+        ),
+        name="sum_everywhere",
+    )(packed).reshape(blocks * each, width)
+    result, start = [], 0
+    for part in parts:
+        result.append(summed[start : start + part.shape[0]].astype(jnp.float32))
+        start += part.shape[0]
+    return result
 
 
 def crps_slope(owned, everyone, aimed):
@@ -121,19 +247,25 @@
     ).astype(jnp.bfloat16)
     mirrored = band_matrix(taps, local, True)
     beside_all = padded_2(dfilt, (("space", 3),), reach)
-    placed = jnp.zeros((members_here, rows + 2, local, channels), jnp.float32)
-    for shift_row in range(3):
-        placed = placed.at[:, shift_row : shift_row + rows].add(
-            jnp.einsum(
-                "kijp,kmipc->mijc",
-                mirrored[:, :, shift_row],
-                beside_all,
-                preferred_element_type=jnp.float32,
-            )
-        )
-    spread_back = placed[:, 1 : rows + 1]
+    placed = jnp.einsum(
+        "kiajp,kmipc->amijc", mirrored, beside_all, preferred_element_type=jnp.float32
+    )
+    spread_back = placed[1]
+    spread_back = spread_back + jnp.pad(placed[0, :, 1:], ((0, 0), (0, 1), (0, 0), (0, 0)))
+    spread_back = spread_back + jnp.pad(placed[2, :, :-1], ((0, 0), (1, 0), (0, 0), (0, 0)))
     grad_input = (dgrad.astype(jnp.float32) + spread_back).astype(jnp.bfloat16)
-    sums = lax.psum((disco_part, up_part, down_part, gain_part), ("ens", "space"))
+    hidden_units = up_part.shape[1]
+    cuts = range(0, hidden_units, channels)
+    pieces = [disco_part.reshape(-1, channels)]
+    pieces += [up_part[:, cut : cut + channels] for cut in cuts]
+    pieces += [down_part, gain_part[None]]
+    summed = sum_everywhere(pieces)
+    sums = (
+        summed[0].reshape(disco_part.shape),
+        jnp.concatenate(summed[1:-2], axis=1),
+        summed[-2],
+        summed[-1][0],
+    )
     factor = 1.0 / math.sqrt(
         members_here * lax.axis_size("ens") * rows * local * lax.axis_size("space")
     )

time: 267 us -> 179 us (0.67)
  waiting for transfers between devices: 116 us -> 61.4 us
  blocking collectives: 38 us -> 0 us
  local copies, waits for them, and re-layouts: 38.9 us -> 7.53 us
  Pallas kernels: 0 us -> 30 us
  matrix products: 29.7 us -> 37.9 us
    psum x1 -> x0, waiting for transfers between devices: 81.3 us -> none  [body(): lax.psum((disco_part, up_part, down_part, gain_part), ('ens', 'space'))]
    psum x1 -> x0, blocking collectives: 38 us -> none  [body(): lax.psum((disco_part, up_part, down_part, gain_part), ('ens', 'space'))]
    gather x4 -> x0, local copies, waits for them, and re-layouts: 30.1 us -> none  [band_matrix(): picked = jnp.take(taps, jnp.clip(offset, 0, count - 1), axis=3)]
    pallas_call x0 -> x1, Pallas kernels: none -> 30 us  [sum_everywhere(): pl.pallas_call(functools.partial(sum_kernel, members, halves), out_shape=...]
    all_gather x1, waiting for transfers between devices: 34.3 us -> 52 us  [body(): everyone = lax.all_gather(output, 'ens', axis=0, tiled=True)]
    dot_general x3 -> x1, matrix products: 9.11 us -> 17.5 us  [body(): jnp.einsum('kiajp,kmipc->amijc', mirrored, beside_all, preferred_element_...]
    ppermute x2, waiting for transfers between devices: 0.01 us -> 6.93 us  [padded_2(): lax.ppermute(lax.slice_in_dim(block, 0, width, axis=dim), axis, backward)]
    unnamed x40 -> x90, local copies, waits for them, and re-layouts: 6.01 us -> 3.64 us
  transfers between devices with their start and end apart: 6 -> 5, of which waited for: 2 -> 4; matrix products, arithmetic and copies ran while one was open for 18% -> 6% of each run, Pallas kernels for 0% -> 0%
where the time goes in v1:
time: 179 us
  waiting for transfers between devices  61.4 us (34%)
  matrix products  37.9 us (21%)
  Pallas kernels  30 us (17%)
  other arithmetic  21.1 us (12%)
  between operations  14.8 us (8%)
  local copies, waits for them, and re-layouts  7.53 us (4%)
  starting transfers between devices  5.87 us (3%)
    all_gather x1, waiting for transfers between devices, body(): everyone = lax.all_gather(output, 'ens', axis=0, tiled=True)  52 us
    pallas_call x1, Pallas kernels, sum_everywhere(): pl.pallas_call(functools.partial(sum_kernel, members, halves), out_shape=...  30 us
    dot_general x1, matrix products, body(): jnp.einsum('kiajp,kmipc->amijc', mirrored, beside_all, preferred_element_...  17.5 us
    ppermute x2, waiting for transfers between devices, padded_2(): lax.ppermute(lax.slice_in_dim(block, 0, width, axis=dim), axis, backward)  6.93 us
    ppermute x2, starting transfers between devices, padded_2(): lax.ppermute(lax.slice_in_dim(block, 0, width, axis=dim), axis, backward)  5.83 us
    unnamed x90, local copies, waits for them, and re-layouts  3.64 us
  transfers between devices with their start and end apart: 5, of which 4 were waited for; matrix products, arithmetic and copies ran while one was open for 6% of the time, Pallas kernels for 0%

profile of v1, /device:TPU:0, one launch (start us, length us, event | category | flops | bytes accessed | tf_op | source)
XLA Modules:
  0.0 178.6 jit_solution(1233984280971362311)
XLA Ops:
  7.2 1.2 fusion.116
  8.5 4.5 %collective-permute-start.1 = (bf16[2,32,4,256]{3,2,0,1:T(4,128)(2,1)S(1)}, bf16[2,32,4,256]{3,2,0,1:T(4,128)(2,1)S(1)}, u32[]{:S(2)}, u32[]{:S(2)}) collective-permute-start(bf16[2,32,4,256]{3,2,0,1:T(4,128)(2,1)S(1)} %get-tuple-element.14), channel_id=1, source_target_pairs={{1,0},{2,1},{3,2},{4,3},{5,4},{6,5},{7,6},{0,7},{9,8},{10,9},{11,1... | collective-permute-start | bytes 393224 | tf_op jit(solution)/shard_map/ppermute | solution.py:24
  13.9 0.8 broadcast_select_fusion
  15.8 3.2 %select_select_fusion = bf16[3,32,3,32,40]{4,3,0,1,2:T(8,128)(2,1)S(1)} fusion(pred[32,40]{1,0:T(8,128)(4,1)S(1)} %get-tuple-element.42, pred[32,40]{1,0:T(8,128)(4,1)S(1)} %get-tuple-element.43, pred[32,40]{1,0:T(8,128)(4,1)S(1)} %get-tuple-element.44, pred[32,40]{1,0:T(8,128)(4,1)S(1)} %get-tuple-element.45, pred[32,40]{1,0:T(8,128)(4,1)S(1)} %get-tuple-element.46, ...), kind=kLoop, calls=%fused_computation.37 | loop fusion | flops 3317760 | bytes 753984 | tf_op jit(solution)/shard_map/jit(_where)/select_n | solution.py:67
  19.2 0.8 pad_maximum_fusion
  20.1 0.9 fusion.47
  21.1 0.9 fusion.50
  22.0 1.3 fusion.15
  23.4 1.1 fusion.42
  25.0 3.2 %multiply_convert_fusion = (bf16[2,32,32,512]{3,2,1,0:T(8,128)(2,1)S(1)}, f32[2,32,32,512]{3,2,1,0:T(8,128)}) fusion(bf16[256,512]{1,0:T(8,128)(2,1)S(1)} %copy-done.17, f32[2,32,32,256,1]{3,2,4,1,0:T(8,128)S(1)} %get-tuple-element.36, f32[256]{0:T(256)S(1)} %copy-done.37, f32[2,32,32]{2,1,0:T(8,128)S(1)} %add_rsqrt_fusion), kind=kOutput, calls=%fused_computation.15 | convolution fusion | flops 547880960 | bytes 8659968 | tf_op jit(solution)/shard_map/mijc,cf->mijf/dot_general | solution.py:222
  28.3 2.4 %fusion.118 = (f32[2,32,32,256]{3,2,1,0:T(8,128)}, bf16[2,32,32,256]{3,2,1,0:T(8,128)(2,1)}) fusion(bf16[2,32,32,512]{3,2,1,0:T(8,128)(2,1)S(1)} %get-tuple-element.37, bf16[512,256]{1,0:T(8,128)(2,1)S(1)} %copy-done.15, bf16[2,32,32,256]{3,2,1,0:T(8,128)(2,1)S(1)} %copy-done.2), kind=kOutput, calls=%fused_computation.156 | convolution fusion | flops 538968064 | bytes 6553600 | tf_op jit(solution)/shard_map/mijf,fc->mijc/dot_general | solution.py:226
  30.7 1.2 convert_element_type.113
  32.5 52.0 %all-gather.2.cloned.1.call-done = bf16[8,32,32,256]{3,2,1,0:T(8,128)(2,1)} async-done(((bf16[2,32,32,256]{3,2,1,0:T(8,128)(2,1)}), bf16[8,32,32,256]{3,2,1,0:T(8,128)(2,1)}) %all-gather.2.cloned.1.call-update) | async-done | bytes 4194320 | tf_op jit(solution)/shard_map/all_gather | solution.py:228
  84.6 3.4 %convert_element_type.114 = f32[8,32,32,256]{3,2,1,0:T(8,128)S(1)} convert(bf16[8,32,32,256]{3,2,1,0:T(8,128)(2,1)} %all-gather.2.cloned.1.call-done) | non-fusion elementwise | flops 2097152 | bytes 12582912 | tf_op jit(solution)/shard_map/convert_element_type | solution.py:195
  88.0 3.5 %fusion.2 = f32[2,32,32,256]{3,2,1,0:T(8,128)S(1)} fusion(f32[8,32,32,256]{3,2,1,0:T(8,128)S(1)} %convert_element_type.114, f32[2,32,32,256]{3,2,1,0:T(8,128)S(1)} %copy-done.4), kind=kLoop, calls=%fused_computation.4 | loop fusion | flops 20447232 | bytes 12582912 | tf_op jit(solution)/shard_map/reduce_sum | solution.py:195
  92.5 1.7 copy-done.44
  94.2 2.9 %fusion.9 = bf16[2,32,32,512]{3,2,1,0:T(8,128)(2,1)S(1)} fusion(f32[2,32,32,512]{3,2,1,0:T(8,128)S(1)} %copy-done.44, bf16[2,32,32,256]{3,2,1,0:T(8,128)(2,1)S(1)} %subtract_convert_fusion, bf16[512,256]{1,0:T(8,128)(2,1)S(1)} %copy-done.16), kind=kOutput, calls=%fused_computation.14 | convolution fusion | flops 558891008 | bytes 7602176 | tf_op jit(solution)/shard_map/mijc,fc->mijf/dot_general | solution.py:231
  97.2 1.0 multiply_reduce_fusion
  98.2 0.9 multiply_convert_fusion.1
  99.1 2.7 %convert_bitcast_fusion = bf16[3,2,32,32,256]{4,3,0,2,1:T(8,128)(2,1)} fusion(bf16[2,32,32,256]{3,2,1,0:T(8,128)(2,1)S(1)} %multiply_convert_fusion.1, bf16[3,256,256]{2,1,0:T(8,128)(2,1)S(1)} %copy-done), kind=kOutput, calls=%fused_computation.25 | convolution fusion | flops 806879232 | bytes 4587520 | tf_op jit(solution)/shard_map/mijd,kcd->kmijc/dot_general | solution.py:245
  101.8 1.8 %fusion.56 = bf16[3,256,256]{2,1,0:T(8,128)(2,1)} fusion(bf16[3,2,32,32,256]{4,3,0,1,2:T(8,128)(2,1)S(1)} %copy-done.9, bf16[2,32,32,256]{3,2,1,0:T(8,128)(2,1)S(1)} %multiply_convert_fusion.1), kind=kOutput, calls=%fused_computation.78 | convolution fusion | flops 805502976 | bytes 4587520 | tf_op jit(solution)/shard_map/kmijc,mijd->kcd/dot_general | solution.py:242
  103.6 1.4 fusion.66
  105.2 0.8 fusion.63
  106.9 30.0 %sum_everywhere.1 = bf16[32,64,256]{2,1,0:T(8,128)(2,1)S(1)} custom-call(bf16[32,64,256]{2,1,0:T(8,128)(2,1)S(1)} %bitcast.171), custom_call_target="tpu_custom_call" | custom-call | tf_op jit(solution)/shard_map/sum_everywhere/pallas_call | solution.py:166
  137.0 0.8 convert_multiply_fusion.1
  138.2 1.3 collective-permute-start.3
  140.0 0.9 convert_multiply_fusion.2
  140.9 1.0 convert_multiply_fusion
  141.9 6.9 %collective-permute-done.3 = bf16[3,2,32,4,256]{4,3,0,2,1:T(4,128)(2,1)S(1)} collective-permute-done((bf16[3,2,32,4,256]{4,3,0,2,1:T(4,128)(2,1)S(1)}, bf16[3,2,32,4,256]{4,3,0,2,1:T(4,128)(2,1)S(1)}, u32[]{:S(2)}, u32[]{:S(2)}) %collective-permute-start.3) | collective-permute-done | bytes 393248 | tf_op jit(solution)/shard_map/ppermute | solution.py:24
  148.8 2.3 %collective-permute-done.2 = bf16[3,2,32,4,256]{4,3,0,2,1:T(4,128)(2,1)S(1)} collective-permute-done((bf16[3,2,32,4,256]{4,3,0,2,1:T(4,128)(2,1)S(1)}, bf16[3,2,32,4,256]{4,3,0,2,1:T(4,128)(2,1)S(1)}, u32[]{:S(2)}, u32[]{:S(2)}) %collective-permute-start.2) | collective-permute-done | bytes 393248 | tf_op jit(solution)/shard_map/ppermute | solution.py:21
  151.2 17.5 %fusion.18 = f32[3,2,32,32,256]{4,3,2,1,0:T(8,128)S(1)} fusion(bf16[3,2,32,4,256]{4,3,0,2,1:T(4,128)(2,1)S(1)} %collective-permute-done.3, bf16[3,2,32,32,256]{4,3,0,2,1:T(8,128)(2,1)S(1)} %copy-done.5, bf16[3,2,32,4,256]{4,3,0,2,1:T(4,128)(2,1)S(1)} %collective-permute-done.2, pred[32,40]{1,0:T(8,128)(4,1)S(1)} %get-tuple-element.27, ...), kind=kOutput, calls=%fused_computation.26 | convolution fusion | flops 392601600 | bytes 10240320 | tf_op jit(solution)/shard_map/kiajp,kmipc->amijc/dot_general | solution.py:250
  169.9 1.8 %fusion.41 = bf16[2,32,32,256]{3,2,1,0:T(8,128)(2,1)} fusion(f32[3,2,32,32,256]{4,3,2,1,0:T(8,128)S(1)} %fusion.18, f32[2,31,32,256]{3,2,1,0:T(8,128)S(1)} %get-tuple-element.8, f32[2,31,32,256]{3,2,1,0:T(8,128)S(1)} %get-tuple-element.7, bf16[2,32,32,256]{3,2,1,0:T(8,128)(2,1)S(1)} %copy-done.7), kind=kLoop, calls=%fused_computation.51 | loop fusion | flops 2621440 | bytes 8257536 | tf_op jit(solution)/shard_map/convert_element_type | solution.py:256
  (125 shorter events, 7.6 us)
Async XLA Ops:
  7.2 16.2 %copy-start = (bf16[3,256,256]{2,1,0:T(8,128)(2,1)S(1)}, bf16[3,256,256]{2,1,0:T(8,128)(2,1)}, u32[]{:S(2)}) copy-start(bf16[3,256,256]{2,1,0:T(8,128)(2,1)} %param.14) | copy-start | bytes 1179652
  7.2 12.0 %copy-start.2 = (bf16[2,32,32,256]{3,2,1,0:T(8,128)(2,1)S(1)}, bf16[2,32,32,256]{3,2,1,0:T(8,128)(2,1)}, u32[]{:S(2)}) copy-start(bf16[2,32,32,256]{3,2,1,0:T(8,128)(2,1)} %param.9) | copy-start | bytes 3145732
  7.2 77.4 %all-gather.2.cloned.1.call-start = ((), (), s32[]{:S(2)}) async-start(), calls=%async_computation | async-start | bytes 5242880 | tf_op jit(solution)/shard_map/all_gather | solution.py:228
  8.5 10.5 %collective-permute-start.1 = (bf16[2,32,4,256]{3,2,0,1:T(4,128)(2,1)S(1)}, bf16[2,32,4,256]{3,2,0,1:T(4,128)(2,1)S(1)}, u32[]{:S(2)}, u32[]{:S(2)}) collective-permute-start(bf16[2,32,4,256]{3,2,0,1:T(4,128)(2,1)S(1)} %get-tuple-element.14), channel_id=1, source_target_pairs={{1,0},{2,1},{3,2},{4,3},{5,4},{6,5},{7,6},{0,7},{9,8},{10,9},{11,1... | collective-permute-start | bytes 393224 | tf_op jit(solution)/shard_map/ppermute | solution.py:24
  13.0 6.2 %collective-permute-start = (bf16[2,32,4,256]{3,2,0,1:T(4,128)(2,1)S(1)}, bf16[2,32,4,256]{3,2,0,1:T(4,128)(2,1)S(1)}, u32[]{:S(2)}, u32[]{:S(2)}) collective-permute-start(bf16[2,32,4,256]{3,2,0,1:T(4,128)(2,1)S(1)} %get-tuple-element.13), channel_id=1, source_target_pairs={{0,1},{1,2},{2,3},{3,4},{4,5},{5,6},{6,7},{7,0},{8,9},{9,10},{10,1... | collective-permute-start | bytes 393224 | tf_op jit(solution)/shard_map/ppermute | solution.py:21
  14.8 5.3 %copy-start.19 = (bf16[3,32,3]{0,1,2:T(8,128)(2,1)}, bf16[3,32,3]{0,1,2:T(8,128)(2,1)S(1)}, u32[]{:S(2)}) copy-start(bf16[3,32,3]{0,1,2:T(8,128)(2,1)S(1)} %copy.69) | copy-start | bytes 1732
  14.9 5.2 %copy-start.21 = (bf16[3,32,3]{0,1,2:T(8,128)(2,1)}, bf16[3,32,3]{0,1,2:T(8,128)(2,1)S(1)}, u32[]{:S(2)}) copy-start(bf16[3,32,3]{0,1,2:T(8,128)(2,1)S(1)} %copy.68) | copy-start | bytes 1732
  15.0 5.1 %copy-start.23 = (bf16[3,32,3]{0,1,2:T(8,128)(2,1)}, bf16[3,32,3]{0,1,2:T(8,128)(2,1)S(1)}, u32[]{:S(2)}) copy-start(bf16[3,32,3]{0,1,2:T(8,128)(2,1)S(1)} %copy.67) | copy-start | bytes 1732
  15.1 5.0 %copy-start.25 = (bf16[3,32,3]{0,1,2:T(8,128)(2,1)}, bf16[3,32,3]{0,1,2:T(8,128)(2,1)S(1)}, u32[]{:S(2)}) copy-start(bf16[3,32,3]{0,1,2:T(8,128)(2,1)S(1)} %copy.66) | copy-start | bytes 1732
  15.3 4.8 %copy-start.27 = (bf16[3,32,3]{0,1,2:T(8,128)(2,1)}, bf16[3,32,3]{0,1,2:T(8,128)(2,1)S(1)}, u32[]{:S(2)}) copy-start(bf16[3,32,3]{0,1,2:T(8,128)(2,1)S(1)} %copy.65) | copy-start | bytes 1732
  15.4 4.7 %copy-start.29 = (bf16[3,32,3]{0,1,2:T(8,128)(2,1)}, bf16[3,32,3]{0,1,2:T(8,128)(2,1)S(1)}, u32[]{:S(2)}) copy-start(bf16[3,32,3]{0,1,2:T(8,128)(2,1)S(1)} %copy.64) | copy-start | bytes 1732
  15.5 4.6 %copy-start.31 = (bf16[3,32,3]{0,1,2:T(8,128)(2,1)}, bf16[3,32,3]{0,1,2:T(8,128)(2,1)S(1)}, u32[]{:S(2)}) copy-start(bf16[3,32,3]{0,1,2:T(8,128)(2,1)S(1)} %copy.63) | copy-start | bytes 1732
  15.6 4.5 %copy-start.33 = (bf16[3,32,3]{0,1,2:T(8,128)(2,1)}, bf16[3,32,3]{0,1,2:T(8,128)(2,1)S(1)}, u32[]{:S(2)}) copy-start(bf16[3,32,3]{0,1,2:T(8,128)(2,1)S(1)} %copy.62) | copy-start | bytes 1732
  92.2 12.8 %copy-start.6 = (bf16[2,32,32,256]{3,2,1,0:T(8,128)(2,1)}, bf16[2,32,32,256]{3,2,1,0:T(8,128)(2,1)S(1)}, u32[]{:S(2)}) copy-start(bf16[2,32,32,256]{3,2,1,0:T(8,128)(2,1)S(1)} %subtract_convert_fusion) | copy-start | bytes 3145732
  106.9 31.0 %copy-start.5 = (bf16[3,2,32,32,256]{4,3,0,2,1:T(8,128)(2,1)S(1)}, bf16[3,2,32,32,256]{4,3,0,2,1:T(8,128)(2,1)}, u32[]{:S(2)}) copy-start(bf16[3,2,32,32,256]{4,3,0,2,1:T(8,128)(2,1)} %convert_bitcast_fusion) | copy-start | bytes 9437188
  136.8 14.2 %copy-start.20 = (bf16[3,32,3]{0,1,2:T(8,128)(2,1)S(1)}, bf16[3,32,3]{0,1,2:T(8,128)(2,1)}, u32[]{:S(2)}) copy-start(bf16[3,32,3]{0,1,2:T(8,128)(2,1)} %copy-done.19) | copy-start | bytes 1732
  136.9 14.2 %copy-start.22 = (bf16[3,32,3]{0,1,2:T(8,128)(2,1)S(1)}, bf16[3,32,3]{0,1,2:T(8,128)(2,1)}, u32[]{:S(2)}) copy-start(bf16[3,32,3]{0,1,2:T(8,128)(2,1)} %copy-done.21) | copy-start | bytes 1732
  136.9 14.2 %copy-start.24 = (bf16[3,32,3]{0,1,2:T(8,128)(2,1)S(1)}, bf16[3,32,3]{0,1,2:T(8,128)(2,1)}, u32[]{:S(2)}) copy-start(bf16[3,32,3]{0,1,2:T(8,128)(2,1)} %copy-done.23) | copy-start | bytes 1732
  136.9 14.2 %copy-start.26 = (bf16[3,32,3]{0,1,2:T(8,128)(2,1)S(1)}, bf16[3,32,3]{0,1,2:T(8,128)(2,1)}, u32[]{:S(2)}) copy-start(bf16[3,32,3]{0,1,2:T(8,128)(2,1)} %copy-done.25) | copy-start | bytes 1732
  136.9 14.2 %copy-start.28 = (bf16[3,32,3]{0,1,2:T(8,128)(2,1)S(1)}, bf16[3,32,3]{0,1,2:T(8,128)(2,1)}, u32[]{:S(2)}) copy-start(bf16[3,32,3]{0,1,2:T(8,128)(2,1)} %copy-done.27) | copy-start | bytes 1732
  136.9 14.2 %copy-start.30 = (bf16[3,32,3]{0,1,2:T(8,128)(2,1)S(1)}, bf16[3,32,3]{0,1,2:T(8,128)(2,1)}, u32[]{:S(2)}) copy-start(bf16[3,32,3]{0,1,2:T(8,128)(2,1)} %copy-done.29) | copy-start | bytes 1732
  136.9 14.2 %copy-start.32 = (bf16[3,32,3]{0,1,2:T(8,128)(2,1)S(1)}, bf16[3,32,3]{0,1,2:T(8,128)(2,1)}, u32[]{:S(2)}) copy-start(bf16[3,32,3]{0,1,2:T(8,128)(2,1)} %copy-done.31) | copy-start | bytes 1732
  136.9 14.2 %copy-start.34 = (bf16[3,32,3]{0,1,2:T(8,128)(2,1)S(1)}, bf16[3,32,3]{0,1,2:T(8,128)(2,1)}, u32[]{:S(2)}) copy-start(bf16[3,32,3]{0,1,2:T(8,128)(2,1)} %copy-done.33) | copy-start | bytes 1732
  136.9 14.2 %copy-start.36 = (bf16[3,32,3]{0,1,2:T(8,128)(2,1)S(1)}, bf16[3,32,3]{0,1,2:T(8,128)(2,1)}, u32[]{:S(2)}) copy-start(bf16[3,32,3]{0,1,2:T(8,128)(2,1)} %copy-done.35) | copy-start | bytes 1732
  136.9 14.2 %copy-start.38 = (pred[32,40]{1,0:T(8,128)(4,1)S(1)}, pred[32,40]{1,0:T(8,128)(4,1)}, u32[]{:S(2)}) copy-start(pred[32,40]{1,0:T(8,128)(4,1)} %get-tuple-element.29) | copy-start | bytes 3844
  136.9 14.2 %copy-start.39 = (pred[32,40]{1,0:T(8,128)(4,1)S(1)}, pred[32,40]{1,0:T(8,128)(4,1)}, u32[]{:S(2)}) copy-start(pred[32,40]{1,0:T(8,128)(4,1)} %get-tuple-element.30) | copy-start | bytes 3844
  137.0 14.2 %copy-start.40 = (pred[32,40]{1,0:T(8,128)(4,1)S(1)}, pred[32,40]{1,0:T(8,128)(4,1)}, u32[]{:S(2)}) copy-start(pred[32,40]{1,0:T(8,128)(4,1)} %get-tuple-element.31) | copy-start | bytes 3844
  137.0 14.2 %copy-start.41 = (pred[32,40]{1,0:T(8,128)(4,1)S(1)}, pred[32,40]{1,0:T(8,128)(4,1)}, u32[]{:S(2)}) copy-start(pred[32,40]{1,0:T(8,128)(4,1)} %get-tuple-element.32) | copy-start | bytes 3844
  137.0 14.2 %copy-start.42 = (pred[32,40]{1,0:T(8,128)(4,1)S(1)}, pred[32,40]{1,0:T(8,128)(4,1)}, u32[]{:S(2)}) copy-start(pred[32,40]{1,0:T(8,128)(4,1)} %get-tuple-element.33) | copy-start | bytes 3844
  137.0 14.2 %copy-start.43 = (pred[32,40]{1,0:T(8,128)(4,1)S(1)}, pred[32,40]{1,0:T(8,128)(4,1)}, u32[]{:S(2)}) copy-start(pred[32,40]{1,0:T(8,128)(4,1)} %get-tuple-element.34) | copy-start | bytes 3844
  138.2 10.6 %collective-permute-start.3 = (bf16[3,2,32,4,256]{4,3,0,2,1:T(4,128)(2,1)S(1)}, bf16[3,2,32,4,256]{4,3,0,2,1:T(4,128)(2,1)S(1)}, u32[]{:S(2)}, u32[]{:S(2)}) collective-permute-start(bf16[3,2,32,4,256]{4,3,0,2,1:T(4,128)(2,1)S(1)} %get-tuple-element.10), channel_id=1, source_target_pairs={{1,0},{2,1},{3,2},{4,3},{5,4},{6,5},{7,6},{0,7},{9,8},{10,9},{11,1... | collective-permute-start | bytes 1179656 | tf_op jit(solution)/shard_map/ppermute | solution.py:24
  139.5 11.6 %collective-permute-start.2 = (bf16[3,2,32,4,256]{4,3,0,2,1:T(4,128)(2,1)S(1)}, bf16[3,2,32,4,256]{4,3,0,2,1:T(4,128)(2,1)S(1)}, u32[]{:S(2)}, u32[]{:S(2)}) collective-permute-start(bf16[3,2,32,4,256]{4,3,0,2,1:T(4,128)(2,1)S(1)} %get-tuple-element.9), channel_id=1, source_target_pairs={{0,1},{1,2},{2,3},{3,4},{4,5},{5,6},{6,7},{7,0},{8,9},{9,10},{10,1... | collective-permute-start | bytes 1179656 | tf_op jit(solution)/shard_map/ppermute | solution.py:21
  (18 other events, 43.7 us)
Sparse Core Ops, SparseCore 0:
  30.8 53.7 all-gather.1

commit v2 on v1

--- a/solution.py
+++ b/solution.py
@@ -180,6 +180,7 @@
         compiler_params=pltpu.CompilerParams(
             collective_id=1, has_side_effects=True, vmem_limit_bytes=24 * 1024 * 1024
         ),
+        cost_estimate=pl.CostEstimate(flops=3 * 10**10, bytes_accessed=2 * 10**6, transcendentals=0),
         name="sum_everywhere",
     )(packed).reshape(blocks * each, width)
     result, start = [], 0
@@ -189,11 +190,103 @@
     return result
 
 
-def crps_slope(owned, everyone, aimed):
-    mine = owned.astype(jnp.float32)
-    miss = slope_abs(mine - aimed.astype(jnp.float32))
-    spread = jnp.sum(slope_abs(mine[:, None] - everyone.astype(jnp.float32)[None]), axis=1)
-    return (miss - spread / (everyone.shape[0] - 1)).astype(jnp.bfloat16)
+def crps_kernel(devices, groups, mine_ref, aimed_ref, slope_ref, held, back, out_send, out_recv, back_send, back_recv):
+    ens, space = lax.axis_index("ens"), lax.axis_index("space")
+    here, rows, local, channels = mine_ref.shape
+    share = rows // devices
+    few = share // groups
+    ahead = [(lax.rem(ens + d, devices), space) for d in range(1, devices)]
+    behind = [(lax.rem(ens + devices - d, devices), space) for d in range(1, devices)]
+    barrier = pltpu.get_barrier_semaphore()
+    for peer in ahead:
+        pl.semaphore_signal(barrier, inc=1, device_id=peer, device_id_type=MESH)
+    pl.semaphore_wait(barrier, devices - 1)
+
+    going = []
+    for group in range(groups):
+        for d in range(devices - 1):
+            copy = pltpu.make_async_remote_copy(
+                src_ref=mine_ref.at[:, pl.ds(ahead[d][0] * share + group * few, few)],
+                dst_ref=held.at[d, group],
+                send_sem=out_send.at[d, group],
+                recv_sem=out_recv.at[d, group],
+                device_id=ahead[d],
+                device_id_type=MESH,
+            )
+            copy.start()
+            going.append(copy)
+
+    tall, wide = 16, 128
+    tiles = local // tall
+    count = here * devices
+    coming = []
+    for group in range(groups):
+        for d in range(devices - 1):
+            going[group * (devices - 1) + d].wait_recv()
+        first = ens * share + group * few
+
+        def tile(step, carry):
+            row = step // tiles
+            lon = pl.ds(pl.multiple_of(lax.rem(step, tiles) * tall, tall), tall)
+            for cut in range(0, channels, wide):
+                part = slice(cut, cut + wide)
+                values = [mine_ref[m, first + row, lon, part].astype(jnp.float32) for m in range(here)]
+                for d in range(devices - 1):
+                    values += [held[d, group, m, row, lon, part].astype(jnp.float32) for m in range(here)]
+                spread = [jnp.zeros((tall, wide), jnp.float32) for _ in range(count)]
+                for m in range(count):
+                    for n in range(m + 1, count):
+                        pair = slope_abs(values[m] - values[n])
+                        spread[m] = spread[m] + pair
+                        spread[n] = spread[n] - pair
+                goal = aimed_ref[first + row, lon, part].astype(jnp.float32)
+                for m in range(count):
+                    slope = slope_abs(values[m] - goal) - spread[m] * (1.0 / (count - 1))
+                    slope = slope.astype(jnp.bfloat16)
+                    if m < here:
+                        slope_ref[m, first + row, lon, part] = slope
+                    else:
+                        back[m // here - 1, group, m % here, row, lon, part] = slope
+            return carry
+
+        lax.fori_loop(0, few * tiles, tile, 0)
+        for d in range(devices - 1):
+            copy = pltpu.make_async_remote_copy(
+                src_ref=back.at[d, group],
+                dst_ref=slope_ref.at[:, pl.ds(first, few)],
+                send_sem=back_send.at[d, group],
+                recv_sem=back_recv.at[d, group],
+                device_id=behind[d],
+                device_id_type=MESH,
+            )
+            copy.start()
+            coming.append((copy, d, group))
+    for copy in going:
+        copy.wait_send()
+    for copy, d, group in coming:
+        copy.wait_send()
+        copy.wait_recv()
+
+
+def crps_slope(owned, aimed):
+    devices = lax.axis_size("ens")
+    here, rows, local, channels = owned.shape
+    share = rows // devices
+    groups = 2 if share % 2 == 0 else 1
+    slots = (devices - 1, groups)
+    whole = pl.BlockSpec(memory_space=pltpu.VMEM)
+    block = slots + (here, share // groups, local, channels)
+    return pl.pallas_call(
+        functools.partial(crps_kernel, devices, groups),
+        out_shape=jax.ShapeDtypeStruct(owned.shape, jnp.bfloat16),
+        in_specs=[whole, whole],
+        out_specs=whole,
+        scratch_shapes=[pltpu.VMEM(block, jnp.bfloat16)] * 2 + [pltpu.SemaphoreType.DMA(slots)] * 4,
+        compiler_params=pltpu.CompilerParams(
+            collective_id=2, has_side_effects=True, vmem_limit_bytes=24 * 1024 * 1024
+        ),
+        name="crps_slope",
+    )(owned, aimed)
 
 
 def body(inputs, target, filter_taps, lon_offset, lon_width, w_disco, w_up, w_down, norm_gain):
@@ -225,8 +318,7 @@
         inputs.astype(jnp.float32)
         + jnp.einsum("mijf,fc->mijc", active, w_down, preferred_element_type=jnp.float32)
     ).astype(jnp.bfloat16)
-    everyone = lax.all_gather(output, "ens", axis=0, tiled=True)
-    dgrad = crps_slope(output, everyone, target[None])
+    dgrad = crps_slope(output, target)
     down_part = jnp.einsum("mijf,mijc->fc", active, dgrad, preferred_element_type=jnp.float32)
     dactive = jnp.einsum("mijc,fc->mijf", dgrad, w_down, preferred_element_type=jnp.float32).astype(
         jnp.bfloat16
@@ -247,12 +339,18 @@
     ).astype(jnp.bfloat16)
     mirrored = band_matrix(taps, local, True)
     beside_all = padded_2(dfilt, (("space", 3),), reach)
-    placed = jnp.einsum(
-        "kiajp,kmipc->amijc", mirrored, beside_all, preferred_element_type=jnp.float32
-    )
+    placed = [
+        jnp.einsum(
+            "kijp,kmipc->mijc",
+            mirrored[:, :, shift_row],
+            beside_all,
+            preferred_element_type=jnp.float32,
+        )
+        for shift_row in range(3)
+    ]
     spread_back = placed[1]
-    spread_back = spread_back + jnp.pad(placed[0, :, 1:], ((0, 0), (0, 1), (0, 0), (0, 0)))
-    spread_back = spread_back + jnp.pad(placed[2, :, :-1], ((0, 0), (1, 0), (0, 0), (0, 0)))
+    spread_back = spread_back + jnp.pad(placed[0][:, 1:], ((0, 0), (0, 1), (0, 0), (0, 0)))
+    spread_back = spread_back + jnp.pad(placed[2][:, :-1], ((0, 0), (1, 0), (0, 0), (0, 0)))
     grad_input = (dgrad.astype(jnp.float32) + spread_back).astype(jnp.bfloat16)
     hidden_units = up_part.shape[1]
     cuts = range(0, hidden_units, channels)

time: 179 us -> 118 us (0.66)
  waiting for transfers between devices: 61.4 us -> 6.01 us
  Pallas kernels: 30 us -> 54.5 us
  matrix products: 37.9 us -> 22.7 us
  between operations: 14.8 us -> 0.97 us
  other arithmetic: 21.1 us -> 14.7 us
  local copies, waits for them, and re-layouts: 7.53 us -> 10.6 us
  starting transfers between devices: 5.87 us -> 8.2 us
    all_gather x1 -> x0, waiting for transfers between devices: 52 us -> none  [body(): everyone = lax.all_gather(output, 'ens', axis=0, tiled=True)]
    pallas_call x0 -> x1, Pallas kernels: none -> 24.9 us  [crps_slope(): pl.pallas_call(functools.partial(crps_kernel, devices, groups), out_shape...]
    dot_general x1 -> x3, matrix products: 17.5 us -> 6.55 us  [body(): jnp.einsum('kijp,kmipc->mijc', mirrored[:, :, shift_row], beside_all, pre...]
    convert_element_type x4 -> x0, other arithmetic: 7.02 us -> none  [the longest x1 3.39 us: crps_slope(): everyone.astype(jnp.float32)[None]]
    ppermute x2, waiting for transfers between devices: 6.93 us -> 0.01 us  [padded_2(): lax.ppermute(lax.slice_in_dim(block, 0, width, axis=dim), axis, backward)]
    concatenate x1, local copies, waits for them, and re-layouts: 0.68 us -> 5.8 us  [sum_everywhere(): jnp.concatenate([part.astype(jnp.bfloat16) for part in parts] + [jnp.zero...]
    select_n x1 -> x2, other arithmetic: 3.23 us -> 8.26 us  [band_matrix(): band = jnp.where(offset == step, taps[:, :, :, step, None, None], band)]
    reduce_sum x1 -> x0, other arithmetic: 3.54 us -> none  [crps_slope(): jnp.sum(slope_abs(mine[:, None] - everyone.astype(jnp.float32)[None]), ax...]
  transfers between devices with their start and end apart: 5 -> 4, of which waited for: 4 -> 1; matrix products, arithmetic and copies ran while one was open for 6% -> 11% of each run, Pallas kernels for 0% -> 0%
where the time goes in v2:
time: 118 us
  Pallas kernels  54.5 us (46%)
  matrix products  22.7 us (19%)
  other arithmetic  14.7 us (12%)
  local copies, waits for them, and re-layouts  10.6 us (9%)
  starting transfers between devices  8.2 us (7%)
  waiting for transfers between devices  6.01 us (5%)
    pallas_call x1, Pallas kernels, sum_everywhere(): pl.pallas_call(functools.partial(sum_kernel, members, halves), out_shape=...  29.6 us
    pallas_call x1, Pallas kernels, crps_slope(): pl.pallas_call(functools.partial(crps_kernel, devices, groups), out_shape...  24.9 us
    select_n x2, other arithmetic, band_matrix(): band = jnp.where(offset == step, taps[:, :, :, step, None, None], band)  8.26 us
    ppermute x2, starting transfers between devices, padded_2(): lax.ppermute(lax.slice_in_dim(block, 0, width, axis=dim), axis, backward)  7.27 us
    dot_general x3, matrix products, body(): jnp.einsum('kijp,kmipc->mijc', mirrored[:, :, shift_row], beside_all, pre...  6.55 us
    ppermute x2, waiting for transfers between devices, padded_2(): lax.ppermute(lax.slice_in_dim(block, block.shape[dim] - width, None, axis...  6 us
    concatenate x1, local copies, waits for them, and re-layouts, sum_everywhere(): jnp.concatenate([part.astype(jnp.bfloat16) for part in parts] + [jnp.zero...  5.8 us
    dot_general x3, matrix products, body(): jnp.einsum('kijp,mipc->kmijc', ahead[:, :, shift_row], padded[:, shift_ro...  3.17 us
  transfers between devices with their start and end apart: 4, of which 1 were waited for; matrix products, arithmetic and copies ran while one was open for 11% of the time, Pallas kernels for 0%

profile of v2, /device:TPU:0, one launch (start us, length us, event | category | flops | bytes accessed | tf_op | source)
XLA Modules:
  0.0 117.6 jit_solution(4579304794056822216)
XLA Ops:
  0.6 1.2 %fusion.75 = (bf16[2,32,4,256]{3,2,0,1:T(4,128)(2,1)S(1)}, bf16[2,32,4,256]{3,2,0,1:T(4,128)(2,1)S(1)}) fusion(bf16[2,32,32,256]{3,2,1,0:T(8,128)(2,1)} %param.9), kind=kLoop, calls=%fused_computation.114 | loop fusion | bytes 524288 | tf_op jit(solution)/shard_map/slice | solution.py:22
  2.3 4.1 %collective-permute-start.1 = (bf16[2,32,4,256]{3,2,0,1:T(4,128)(2,1)S(1)}, bf16[2,32,4,256]{3,2,0,1:T(4,128)(2,1)S(1)}, u32[]{:S(2)}, u32[]{:S(2)}) collective-permute-start(bf16[2,32,4,256]{3,2,0,1:T(4,128)(2,1)S(1)} %get-tuple-element.12), channel_id=1, source_target_pairs={{1,0},{2,1},{3,2},{4,3},{5,4},{6,5},{7,6},{0,7},{9,8},{10,9},{11,1... | collective-permute-start | bytes 393224 | tf_op jit(solution)/shard_map/ppermute | solution.py:24
  6.5 0.8 abs_compare_fusion
  7.3 0.8 broadcast_select_fusion
  9.3 3.2 %select_select_fusion.1 = bf16[3,32,3,32,40]{4,3,0,1,2:T(8,128)(2,1)S(1)} fusion(pred[32,40]{1,0:T(8,128)(4,1)S(1)} %get-tuple-element.38, pred[32,40]{1,0:T(8,128)(4,1)S(1)} %get-tuple-element.39, pred[32,40]{1,0:T(8,128)(4,1)S(1)} %get-tuple-element.40, pred[32,40]{1,0:T(8,128)(4,1)S(1)} %get-tuple-element.41, pred[32,40]{1,0:T(8,128)(4,1)S(1)} %get-tuple-element.42, ...), kind=kLoop, calls=%fused_computation.17 | loop fusion | flops 3317760 | bytes 753984 | tf_op jit(solution)/shard_map/jit(_where)/select_n | solution.py:67
  12.5 5.0 %select_select_fusion = bf16[3,32,3,32,40]{4,3,0,1,2:T(8,128)(2,1)} fusion(pred[32,40]{1,0:T(8,128)(4,1)S(1)} %get-tuple-element.25, pred[32,40]{1,0:T(8,128)(4,1)S(1)} %get-tuple-element.26, pred[32,40]{1,0:T(8,128)(4,1)S(1)} %get-tuple-element.27, pred[32,40]{1,0:T(8,128)(4,1)S(1)} %get-tuple-element.28, pred[32,40]{1,0:T(8,128)(4,1)S(1)} %get-tuple-element.29, ...), kind=kLoop, calls=%fused_computation.16 | loop fusion | flops 3317760 | bytes 753984 | tf_op jit(solution)/shard_map/jit(_where)/select_n | solution.py:67
  17.5 0.8 pad_maximum_fusion.1
  18.4 0.9 fusion.18
  19.3 0.9 fusion.21
  20.3 1.3 %fusion.7 = bf16[3,2,32,32,256]{4,3,0,1,2:T(8,128)(2,1)S(1)} fusion(f32[32,2,256,3,32]{2,4,3,1,0:T(8,128)S(1)} %fusion.18, f32[32,2,256,3,32]{2,4,3,1,0:T(8,128)S(1)} %fusion.21, bf16[3,32,3,32,40]{4,3,0,1,2:T(8,128)(2,1)S(1)} %select_select_fusion.1, bf16[2,32,4,256]{3,2,0,1:T(4,128)(2,1)S(1)} %collective-permute-done.1, ...), kind=kOutput, calls=%fused_computation.12 | convolution fusion | flops 134479872 | bytes 17825792 | tf_op jit(solution)/shard_map/kijp,mipc->kmijc/dot_general | solution.py:304
  21.6 1.1 fusion.13
  22.7 1.7 %multiply_convert_fusion = (bf16[2,32,32,512]{3,2,1,0:T(8,128)(2,1)S(1)}, f32[2,32,32,512]{3,2,1,0:T(8,128)S(1)}) fusion(bf16[256,512]{1,0:T(8,128)(2,1)S(1)} %copy-done.5, f32[2,32,32,256,1]{3,2,4,1,0:T(8,128)S(1)} %get-tuple-element.34, f32[256]{0:T(256)S(1)} %copy-done.6, f32[2,32,32]{2,1,0:T(8,128)S(1)} %add_rsqrt_fusion), kind=kOutput, calls=%fused_computation.10 | convolution fusion | flops 547880960 | bytes 8659968 | tf_op jit(solution)/shard_map/mijc,cf->mijf/dot_general | solution.py:315
  24.4 0.7 add_convert_fusion.1.mine_ref
  25.5 24.9 %crps_slope.1 = bf16[2,32,32,256]{3,2,1,0:T(8,128)(2,1)S(1)} custom-call(bf16[2,32,32,256]{3,2,1,0:T(8,128)(2,1)S(1)} %add_convert_fusion.1.mine_ref, bf16[32,32,256]{2,1,0:T(8,128)(2,1)S(1)} %copy-done.1), custom_call_target="tpu_custom_call" | custom-call | tf_op jit(solution)/shard_map/crps_slope/pallas_call | solution.py:279
  50.3 1.5 %fusion.34 = bf16[512,256]{1,0:T(8,128)(2,1)} fusion(bf16[2,32,32,512]{3,2,1,0:T(8,128)(2,1)S(1)} %get-tuple-element.35, bf16[2,32,32,256]{3,2,1,0:T(8,128)(2,1)S(1)} %crps_slope.1), kind=kOutput, calls=%fused_computation.50 | convolution fusion | flops 537001984 | bytes 3407872 | tf_op jit(solution)/shard_map/mijf,mijc->fc/dot_general | solution.py:322
  51.8 2.9 %fusion.6 = bf16[2,32,32,512]{3,2,1,0:T(8,128)(2,1)S(1)} fusion(f32[2,32,32,512]{3,2,1,0:T(8,128)S(1)} %get-tuple-element.36, bf16[2,32,32,256]{3,2,1,0:T(8,128)(2,1)S(1)} %crps_slope.1, bf16[512,256]{1,0:T(8,128)(2,1)S(1)} %copy-done.4), kind=kOutput, calls=%fused_computation.9 | convolution fusion | flops 558891008 | bytes 7602176 | tf_op jit(solution)/shard_map/mijc,fc->mijf/dot_general | solution.py:323
  54.7 1.4 %fusion.37 = bf16[256,512]{1,0:T(8,128)(2,1)S(1)} fusion(bf16[2,32,32,512]{3,2,1,0:T(8,128)(2,1)S(1)} %fusion.6, f32[2,32,32,256,1]{3,2,4,1,0:T(8,128)S(1)} %get-tuple-element.34, f32[256]{0:T(256)S(1)} %copy-done.6, f32[2,32,32]{2,1,0:T(8,128)S(1)} %add_rsqrt_fusion), kind=kOutput, calls=%fused_computation.51 | convolution fusion | flops 538574848 | bytes 4465664 | tf_op jit(solution)/shard_map/mijc,mijf->cf/dot_general | solution.py:327
  56.2 0.9 multiply_reduce_fusion
  57.1 0.7 fusion.76
  57.8 0.7 multiply_convert_fusion.1
  58.5 1.8 %fusion.27 = bf16[3,256,256]{2,1,0:T(8,128)(2,1)} fusion(bf16[3,2,32,32,256]{4,3,0,1,2:T(8,128)(2,1)S(1)} %fusion.7, bf16[2,32,32,256]{3,2,1,0:T(8,128)(2,1)S(1)} %multiply_convert_fusion.1), kind=kOutput, calls=%fused_computation.47 | convolution fusion | flops 805502976 | bytes 4587520 | tf_op jit(solution)/shard_map/kmijc,mijd->kcd/dot_general | solution.py:334
  60.9 5.8 %concatenate.17 = bf16[2048,256]{1,0:T(8,128)(2,1)S(1)} concatenate(bf16[768,256]{1,0:T(8,128)(2,1)} %bitcast.177, bf16[256,256]{1,0:T(8,128)(2,1)} %get-tuple-element.14, bf16[256,256]{1,0:T(8,128)(2,1)} %get-tuple-element.13, bf16[512,256]{1,0:T(8,128)(2,1)} %fusion.34, bf16[1,256]{1,0:T(2,128)(2,1)S(1)} %convert_element_type.111, bf16[255,256]{1,0:T(8,128)(2,1)} %broadcast_in_dim.213), dimensions={0} | concatenate | bytes 2097152 | tf_op jit(solution)/shard_map/concatenate | solution.py:160
  66.7 29.6 %sum_everywhere.1 = bf16[32,64,256]{2,1,0:T(8,128)(2,1)S(1)} custom-call(bf16[32,64,256]{2,1,0:T(8,128)(2,1)S(1)} %bitcast.171), custom_call_target="tpu_custom_call" | custom-call | flops 30000001024 | bytes 2000000 | tf_op jit(solution)/shard_map/sum_everywhere/pallas_call | solution.py:166
  96.4 0.8 convert_multiply_fusion.1
  97.3 1.0 convert_bitcast_fusion
  99.0 3.2 %collective-permute-start.3 = (bf16[3,2,32,4,256]{4,3,0,2,1:T(4,128)(2,1)S(1)}, bf16[3,2,32,4,256]{4,3,0,2,1:T(4,128)(2,1)S(1)}, u32[]{:S(2)}, u32[]{:S(2)}) collective-permute-start(bf16[3,2,32,4,256]{4,3,0,2,1:T(4,128)(2,1)S(1)} %get-tuple-element.8), channel_id=1, source_target_pairs={{1,0},{2,1},{3,2},{4,3},{5,4},{6,5},{7,6},{0,7},{9,8},{10,9},{11,1... | collective-permute-start | bytes 1179656 | tf_op jit(solution)/shard_map/ppermute | solution.py:24
  102.8 0.9 convert_multiply_fusion.2
  103.6 1.0 convert_multiply_fusion
  104.6 6.0 %collective-permute-done.2 = bf16[3,2,32,4,256]{4,3,0,2,1:T(4,128)(2,1)S(1)} collective-permute-done((bf16[3,2,32,4,256]{4,3,0,2,1:T(4,128)(2,1)S(1)}, bf16[3,2,32,4,256]{4,3,0,2,1:T(4,128)(2,1)S(1)}, u32[]{:S(2)}, u32[]{:S(2)}) %collective-permute-start.2) | collective-permute-done | bytes 393248 | tf_op jit(solution)/shard_map/ppermute | solution.py:21
  110.6 1.8 %convolution_bitcast_fusion.1 = f32[2,32,32,256]{3,2,1,0:T(8,128)S(1)} fusion(bf16[3,32,3,32,40]{4,3,0,1,2:T(8,128)(2,1)S(1)} %copy-done.3, bf16[3,2,32,4,256]{4,3,0,2,1:T(4,128)(2,1)S(1)} %collective-permute-done.3, bf16[3,2,32,32,256]{4,3,0,2,1:T(8,128)(2,1)S(1)} %convert_bitcast_fusion, bf16[3,2,32,4,256]{4,3,0,2,1:T(4,128)(2,1)S(1)} %collective-permute-done.2), kind=kOutput, calls=%fused_computation.35 | convolution fusion | flops 137625600 | bytes 6815744 | tf_op jit(solution)/shard_map/kijp,kmipc->mijc/dot_general | solution.py:343
  112.7 1.9 %convolution_bitcast_fusion = f32[2,32,32,256]{3,2,1,0:T(8,128)S(1)} fusion(bf16[3,32,3,32,40]{4,3,0,1,2:T(8,128)(2,1)S(1)} %copy-done.3, bf16[3,2,32,4,256]{4,3,0,2,1:T(4,128)(2,1)S(1)} %collective-permute-done.3, bf16[3,2,32,32,256]{4,3,0,2,1:T(8,128)(2,1)S(1)} %convert_bitcast_fusion, bf16[3,2,32,4,256]{4,3,0,2,1:T(4,128)(2,1)S(1)} %collective-permute-done.2), kind=kOutput, calls=%fused_computation.34 | convolution fusion | flops 137625600 | bytes 6815744 | tf_op jit(solution)/shard_map/kijp,kmipc->mijc/dot_general | solution.py:343
  114.8 2.8 %fusion.12 = bf16[2,32,32,256]{3,2,1,0:T(8,128)(2,1)} fusion(f32[2,31,32,256]{3,2,1,0:T(8,128)S(1)} %slice.156, f32[2,31,32,256]{3,2,1,0:T(8,128)S(1)} %slice.154, bf16[2,32,32,256]{3,2,1,0:T(8,128)(2,1)S(1)} %crps_slope.1, bf16[3,32,3,32,40]{4,3,0,1,2:T(8,128)(2,1)S(1)} %copy-done.3, bf16[3,2,32,4,256]{4,3,0,2,1:T(4,128)(2,1)S(1)} %collective-permute-done.3, ...), kind=kOutput, calls=%fused_computation.21 | convolution fusion | flops 140247040 | bytes 10878976 | tf_op jit(solution)/shard_map/kijp,kmipc->mijc/dot_general | solution.py:343
  (46 shorter events, 4.5 us)
Async XLA Ops:
  0.6 21.0 %copy-start = (bf16[3,256,256]{2,1,0:T(8,128)(2,1)S(1)}, bf16[3,256,256]{2,1,0:T(8,128)(2,1)}, u32[]{:S(2)}) copy-start(bf16[3,256,256]{2,1,0:T(8,128)(2,1)} %param.14) | copy-start | bytes 1179652
  1.8 15.7 %collective-permute-start = (bf16[2,32,4,256]{3,2,0,1:T(4,128)(2,1)S(1)}, bf16[2,32,4,256]{3,2,0,1:T(4,128)(2,1)S(1)}, u32[]{:S(2)}, u32[]{:S(2)}) collective-permute-start(bf16[2,32,4,256]{3,2,0,1:T(4,128)(2,1)S(1)} %get-tuple-element.11), channel_id=1, source_target_pairs={{0,1},{1,2},{2,3},{3,4},{4,5},{5,6},{6,7},{7,0},{8,9},{9,10},{10,1... | collective-permute-start | bytes 393224 | tf_op jit(solution)/shard_map/ppermute | solution.py:21
  2.3 15.2 %collective-permute-start.1 = (bf16[2,32,4,256]{3,2,0,1:T(4,128)(2,1)S(1)}, bf16[2,32,4,256]{3,2,0,1:T(4,128)(2,1)S(1)}, u32[]{:S(2)}, u32[]{:S(2)}) collective-permute-start(bf16[2,32,4,256]{3,2,0,1:T(4,128)(2,1)S(1)} %get-tuple-element.12), channel_id=1, source_target_pairs={{1,0},{2,1},{3,2},{4,3},{5,4},{6,5},{7,6},{0,7},{9,8},{10,9},{11,1... | collective-permute-start | bytes 393224 | tf_op jit(solution)/shard_map/ppermute | solution.py:24
  9.3 8.3 %copy-start.2 = (bf16[2,32,32,256]{3,2,1,0:T(8,128)(2,1)S(1)}, bf16[2,32,32,256]{3,2,1,0:T(8,128)(2,1)}, u32[]{:S(2)}) copy-start(bf16[2,32,32,256]{3,2,1,0:T(8,128)(2,1)} %param.9) | copy-start | bytes 3145732
  21.6 1.1 copy-start.5
  21.6 1.1 copy-start.6
  22.7 1.7 %copy-start.4 = (bf16[512,256]{1,0:T(8,128)(2,1)S(1)}, bf16[512,256]{1,0:T(8,128)(2,1)}, u32[]{:S(2)}) copy-start(bf16[512,256]{1,0:T(8,128)(2,1)} %param.16) | copy-start | bytes 786436
  24.4 1.0 copy-start.1
  98.3 12.3 %copy-start.3 = (bf16[3,32,3,32,40]{4,3,0,1,2:T(8,128)(2,1)S(1)}, bf16[3,32,3,32,40]{4,3,0,1,2:T(8,128)(2,1)}, u32[]{:S(2)}) copy-start(bf16[3,32,3,32,40]{4,3,0,1,2:T(8,128)(2,1)} %select_select_fusion) | copy-start | bytes 2211844
  98.6 12.0 %collective-permute-start.2 = (bf16[3,2,32,4,256]{4,3,0,2,1:T(4,128)(2,1)S(1)}, bf16[3,2,32,4,256]{4,3,0,2,1:T(4,128)(2,1)S(1)}, u32[]{:S(2)}, u32[]{:S(2)}) collective-permute-start(bf16[3,2,32,4,256]{4,3,0,2,1:T(4,128)(2,1)S(1)} %get-tuple-element.7), channel_id=1, source_target_pairs={{0,1},{1,2},{2,3},{3,4},{4,5},{5,6},{6,7},{7,0},{8,9},{9,10},{10,1... | collective-permute-start | bytes 1179656 | tf_op jit(solution)/shard_map/ppermute | solution.py:21
  99.0 11.6 %collective-permute-start.3 = (bf16[3,2,32,4,256]{4,3,0,2,1:T(4,128)(2,1)S(1)}, bf16[3,2,32,4,256]{4,3,0,2,1:T(4,128)(2,1)S(1)}, u32[]{:S(2)}, u32[]{:S(2)}) collective-permute-start(bf16[3,2,32,4,256]{4,3,0,2,1:T(4,128)(2,1)S(1)} %get-tuple-element.8), channel_id=1, source_target_pairs={{1,0},{2,1},{3,2},{4,3},{5,4},{6,5},{7,6},{0,7},{9,8},{10,9},{11,1... | collective-permute-start | bytes 1179656 | tf_op jit(solution)/shard_map/ppermute | solution.py:24

commit v3 on v2

--- a/solution.py
+++ b/solution.py
@@ -68,14 +68,16 @@
     return band
 
 
-def sum_kernel(members, halves, part_ref, full_ref, sum_core, sum_ens, from_core, from_ens, from_space, send, recv):
+def sum_kernel(members, halves, part_ref, edge_ref, full_ref, beside_ref, sum_core, sum_ens, from_core, from_ens, from_space, send, recv):
     ens, space = lax.axis_index("ens"), lax.axis_index("space")
     core, half = lax.rem(space, 2), space // 2
     other = space + 1 - 2 * core
     ens_peers = [(lax.rem(ens + d, members), space) for d in range(1, members)]
     space_peers = [(ens, lax.rem(half + d, halves) * 2 + core) for d in range(1, halves)]
     barrier = pltpu.get_barrier_semaphore()
-    everyone = [(ens, other)] + ens_peers + space_peers
+    right = (ens, lax.rem(space + 1, 2 * halves))
+    left = (ens, lax.rem(space + 2 * halves - 1, 2 * halves))
+    everyone = [(ens, other), right, left] + ens_peers + space_peers
     for peer in everyone:
         pl.semaphore_signal(barrier, inc=1, device_id=peer, device_id_type=MESH)
     pl.semaphore_wait(barrier, len(everyone))
@@ -92,6 +94,11 @@
         copy.start()
         return copy
 
+    sides = 2 * (members + halves - 1)
+    edges = [
+        move(edge_ref.at[0], beside_ref.at[0], sides, right),
+        move(edge_ref.at[1], beside_ref.at[1], sides + 1, left),
+    ]
     wide = members * halves
     first_core = core * wide
     copies = [move(part_ref.at[pl.ds((1 - core) * wide, wide)], from_core, 0, (ens, other))]
@@ -149,9 +156,11 @@
         copy.wait()
     block = full_ref.at[pl.ds(first_core, wide)]
     move(block, block, back, (ens, other)).wait()
-
-
-def sum_everywhere(parts):
+    for copy in edges:
+        copy.wait()
+
+
+def sum_everywhere(parts, edges):
     members, halves = lax.axis_size("ens"), lax.axis_size("space") // 2
     blocks = 2 * members * halves
     width = parts[0].shape[1]
@@ -162,12 +171,15 @@
         + [jnp.zeros((blocks * each - rows, width), jnp.bfloat16)]
     ).reshape(blocks, each, width)
     whole = pl.BlockSpec(memory_space=pltpu.VMEM)
-    count = 2 * (members + halves - 1)
-    summed = pl.pallas_call(
+    count = 2 * (members + halves - 1) + 2
+    summed, beside = pl.pallas_call(
         functools.partial(sum_kernel, members, halves),
-        out_shape=jax.ShapeDtypeStruct(packed.shape, jnp.bfloat16),
-        in_specs=[whole],
-        out_specs=whole,
+        out_shape=[
+            jax.ShapeDtypeStruct(packed.shape, jnp.bfloat16),
+            jax.ShapeDtypeStruct(edges.shape, jnp.bfloat16),
+        ],
+        in_specs=[whole, whole],
+        out_specs=[whole, whole],
         scratch_shapes=[
             pltpu.VMEM((members * halves, each, width), jnp.bfloat16),
             pltpu.VMEM((halves, each, width), jnp.bfloat16),
@@ -182,12 +194,13 @@
         ),
         cost_estimate=pl.CostEstimate(flops=3 * 10**10, bytes_accessed=2 * 10**6, transcendentals=0),
         name="sum_everywhere",
-    )(packed).reshape(blocks * each, width)
+    )(packed, edges)
+    summed = summed.reshape(blocks * each, width)
     result, start = [], 0
     for part in parts:
         result.append(summed[start : start + part.shape[0]].astype(jnp.float32))
         start += part.shape[0]
-    return result
+    return result, beside
 
 
 def crps_kernel(devices, groups, mine_ref, aimed_ref, slope_ref, held, back, out_send, out_recv, back_send, back_recv):
@@ -337,8 +350,22 @@
     dfilt = jnp.einsum(
         "mijd,kcd->kmijc", dhidden, w_disco, preferred_element_type=jnp.float32
     ).astype(jnp.bfloat16)
+    hidden_units = up_part.shape[1]
+    cuts = range(0, hidden_units, channels)
+    pieces = [disco_part.reshape(-1, channels)]
+    pieces += [up_part[:, cut : cut + channels] for cut in cuts]
+    pieces += [down_part, gain_part[None]]
+    edges = jnp.stack([dfilt[:, :, :, local - reach :], dfilt[:, :, :, :reach]])
+    summed, beside = sum_everywhere(pieces, edges.reshape(2, -1, channels))
+    beside = beside.reshape(edges.shape)
+    beside_all = jnp.concatenate([beside[0], dfilt, beside[1]], axis=3)
+    sums = (
+        summed[0].reshape(disco_part.shape),
+        jnp.concatenate(summed[1:-2], axis=1),
+        summed[-2],
+        summed[-1][0],
+    )
     mirrored = band_matrix(taps, local, True)
-    beside_all = padded_2(dfilt, (("space", 3),), reach)
     placed = [
         jnp.einsum(
             "kijp,kmipc->mijc",
@@ -352,18 +379,6 @@
     spread_back = spread_back + jnp.pad(placed[0][:, 1:], ((0, 0), (0, 1), (0, 0), (0, 0)))
     spread_back = spread_back + jnp.pad(placed[2][:, :-1], ((0, 0), (1, 0), (0, 0), (0, 0)))
     grad_input = (dgrad.astype(jnp.float32) + spread_back).astype(jnp.bfloat16)
-    hidden_units = up_part.shape[1]
-    cuts = range(0, hidden_units, channels)
-    pieces = [disco_part.reshape(-1, channels)]
-    pieces += [up_part[:, cut : cut + channels] for cut in cuts]
-    pieces += [down_part, gain_part[None]]
-    summed = sum_everywhere(pieces)
-    sums = (
-        summed[0].reshape(disco_part.shape),
-        jnp.concatenate(summed[1:-2], axis=1),
-        summed[-2],
-        summed[-1][0],
-    )
     factor = 1.0 / math.sqrt(
         members_here * lax.axis_size("ens") * rows * local * lax.axis_size("space")
     )

time: 118 us -> 111 us (0.941)
  waiting for transfers between devices: 6.01 us -> 0.01 us
  starting transfers between devices: 8.2 us -> 4.61 us
  matrix products: 22.7 us -> 24.7 us
  local copies, waits for them, and re-layouts: 10.6 us -> 9.13 us
  other arithmetic: 14.7 us -> 15.9 us
    ppermute x2 -> x1, waiting for transfers between devices: 6 us -> 0.01 us  [padded_2(): lax.ppermute(lax.slice_in_dim(block, block.shape[dim] - width, None, axis...]
    ppermute x2 -> x1, starting transfers between devices: 7.27 us -> 4.1 us  [padded_2(): lax.ppermute(lax.slice_in_dim(block, 0, width, axis=dim), axis, backward)]
    concatenate x1, local copies, waits for them, and re-layouts: 5.8 us -> 3.34 us  [sum_everywhere(): jnp.concatenate([part.astype(jnp.bfloat16) for part in parts] + [jnp.zero...]
    dot_general x3, matrix products: 6.55 us -> 8.59 us  [body(): jnp.einsum('kijp,kmipc->mijc', mirrored[:, :, shift_row], beside_all, pre...]
  transfers between devices with their start and end apart: 4 -> 2, of which waited for: 1 -> 0; matrix products, arithmetic and copies ran while one was open for 11% -> 10% of each run, Pallas kernels for 0% -> 0%
where the time goes in v3:
time: 111 us; the launch traced here: 110 us
  Pallas kernels  55.1 us (50%)
  matrix products  24.7 us (22%)
  other arithmetic  15.9 us (14%)
  local copies, waits for them, and re-layouts  9.13 us (8%)
  starting transfers between devices  4.61 us (4%)
    pallas_call x1, Pallas kernels, sum_everywhere(): pl.pallas_call(functools.partial(sum_kernel, members, halves), out_shape=...  30.2 us
    pallas_call x1, Pallas kernels, crps_slope(): pl.pallas_call(functools.partial(crps_kernel, devices, groups), out_shape...  24.9 us
    dot_general x3, matrix products, body(): jnp.einsum('kijp,kmipc->mijc', mirrored[:, :, shift_row], beside_all, pre...  8.59 us
    select_n x2, other arithmetic, band_matrix(): band = jnp.where(offset == step, taps[:, :, :, step, None, None], band)  8.27 us
    ppermute x1, starting transfers between devices, padded_2(): lax.ppermute(lax.slice_in_dim(block, 0, width, axis=dim), axis, backward)  4.1 us
    concatenate x1, local copies, waits for them, and re-layouts, sum_everywhere(): jnp.concatenate([part.astype(jnp.bfloat16) for part in parts] + [jnp.zero...  3.34 us
    dot_general x3, matrix products, body(): jnp.einsum('kijp,mipc->kmijc', ahead[:, :, shift_row], padded[:, shift_ro...  3.17 us
    dot_general x1, matrix products, body(): jnp.einsum('mijc,fc->mijf', dgrad, w_down, preferred_element_type=jnp.flo...  2.94 us
  transfers between devices with their start and end apart: 2, of which 0 were waited for; matrix products, arithmetic and copies ran while one was open for 10% of the time, Pallas kernels for 0%

profile of v3, /device:TPU:0, one launch (start us, length us, event | category | flops | bytes accessed | tf_op | source)
XLA Modules:
  0.0 110.5 jit_solution(13358726888982748665)
XLA Ops:
  0.6 1.2 %fusion.75 = (bf16[2,32,4,256]{3,2,0,1:T(4,128)(2,1)S(1)}, bf16[2,32,4,256]{3,2,0,1:T(4,128)(2,1)S(1)}) fusion(bf16[2,32,32,256]{3,2,1,0:T(8,128)(2,1)} %param.9), kind=kLoop, calls=%fused_computation.115 | loop fusion | bytes 524288 | tf_op jit(solution)/shard_map/slice | solution.py:22
  2.3 4.1 %collective-permute-start.1 = (bf16[2,32,4,256]{3,2,0,1:T(4,128)(2,1)S(1)}, bf16[2,32,4,256]{3,2,0,1:T(4,128)(2,1)S(1)}, u32[]{:S(2)}, u32[]{:S(2)}) collective-permute-start(bf16[2,32,4,256]{3,2,0,1:T(4,128)(2,1)S(1)} %get-tuple-element.16), channel_id=1, source_target_pairs={{1,0},{2,1},{3,2},{4,3},{5,4},{6,5},{7,6},{0,7},{9,8},{10,9},{11,1... | collective-permute-start | bytes 393224 | tf_op jit(solution)/shard_map/ppermute | solution.py:24
  6.5 0.8 abs_compare_fusion
  7.3 0.8 broadcast_select_fusion
  9.3 3.2 %select_select_fusion.1 = bf16[3,32,3,32,40]{4,3,0,1,2:T(8,128)(2,1)S(1)} fusion(pred[32,40]{1,0:T(8,128)(4,1)S(1)} %get-tuple-element.44, pred[32,40]{1,0:T(8,128)(4,1)S(1)} %get-tuple-element.45, pred[32,40]{1,0:T(8,128)(4,1)S(1)} %get-tuple-element.46, pred[32,40]{1,0:T(8,128)(4,1)S(1)} %get-tuple-element.47, pred[32,40]{1,0:T(8,128)(4,1)S(1)} %get-tuple-element.48, ...), kind=kLoop, calls=%fused_computation.17 | loop fusion | flops 3317760 | bytes 753984 | tf_op jit(solution)/shard_map/jit(_where)/select_n | solution.py:67
  12.5 5.0 %select_select_fusion = bf16[3,32,3,32,40]{4,3,0,1,2:T(8,128)(2,1)} fusion(pred[32,40]{1,0:T(8,128)(4,1)S(1)} %get-tuple-element.31, pred[32,40]{1,0:T(8,128)(4,1)S(1)} %get-tuple-element.32, pred[32,40]{1,0:T(8,128)(4,1)S(1)} %get-tuple-element.33, pred[32,40]{1,0:T(8,128)(4,1)S(1)} %get-tuple-element.34, pred[32,40]{1,0:T(8,128)(4,1)S(1)} %get-tuple-element.35, ...), kind=kLoop, calls=%fused_computation.16 | loop fusion | flops 3317760 | bytes 753984 | tf_op jit(solution)/shard_map/jit(_where)/select_n | solution.py:67
  17.6 0.8 pad_maximum_fusion.1
  18.4 0.9 fusion.18
  19.3 0.9 fusion.21
  20.3 1.3 %fusion.7 = bf16[3,2,32,32,256]{4,3,0,1,2:T(8,128)(2,1)S(1)} fusion(f32[32,2,256,3,32]{2,4,3,1,0:T(8,128)S(1)} %fusion.18, f32[32,2,256,3,32]{2,4,3,1,0:T(8,128)S(1)} %fusion.21, bf16[3,32,3,32,40]{4,3,0,1,2:T(8,128)(2,1)S(1)} %select_select_fusion.1, bf16[2,32,4,256]{3,2,0,1:T(4,128)(2,1)S(1)} %collective-permute-done.1, ...), kind=kOutput, calls=%fused_computation.12 | convolution fusion | flops 134479872 | bytes 17825792 | tf_op jit(solution)/shard_map/kijp,mipc->kmijc/dot_general | solution.py:317
  21.6 1.1 fusion.13
  22.7 1.6 %multiply_convert_fusion = (bf16[2,32,32,512]{3,2,1,0:T(8,128)(2,1)S(1)}, f32[2,32,32,512]{3,2,1,0:T(8,128)S(1)}) fusion(bf16[256,512]{1,0:T(8,128)(2,1)S(1)} %copy-done.10, f32[2,32,32,256,1]{3,2,4,1,0:T(8,128)S(1)} %get-tuple-element.40, f32[256]{0:T(256)S(1)} %copy-done.11, f32[2,32,32]{2,1,0:T(8,128)S(1)} %add_rsqrt_fusion), kind=kOutput, calls=%fused_computation.10 | convolution fusion | flops 547880960 | bytes 8659968 | tf_op jit(solution)/shard_map/mijc,cf->mijf/dot_general | solution.py:328
  24.4 0.7 add_convert_fusion.1.mine_ref
  25.4 24.9 %crps_slope.1 = bf16[2,32,32,256]{3,2,1,0:T(8,128)(2,1)S(1)} custom-call(bf16[2,32,32,256]{3,2,1,0:T(8,128)(2,1)S(1)} %add_convert_fusion.1.mine_ref, bf16[32,32,256]{2,1,0:T(8,128)(2,1)S(1)} %copy-done.2), custom_call_target="tpu_custom_call" | custom-call | tf_op jit(solution)/shard_map/crps_slope/pallas_call | solution.py:292
  50.3 1.5 %fusion.34 = bf16[512,256]{1,0:T(8,128)(2,1)} fusion(bf16[2,32,32,512]{3,2,1,0:T(8,128)(2,1)S(1)} %get-tuple-element.41, bf16[2,32,32,256]{3,2,1,0:T(8,128)(2,1)S(1)} %crps_slope.1), kind=kOutput, calls=%fused_computation.50 | convolution fusion | flops 537001984 | bytes 3407872 | tf_op jit(solution)/shard_map/mijf,mijc->fc/dot_general | solution.py:335
  51.8 2.9 %fusion.6 = bf16[2,32,32,512]{3,2,1,0:T(8,128)(2,1)S(1)} fusion(f32[2,32,32,512]{3,2,1,0:T(8,128)S(1)} %get-tuple-element.42, bf16[2,32,32,256]{3,2,1,0:T(8,128)(2,1)S(1)} %crps_slope.1, bf16[512,256]{1,0:T(8,128)(2,1)S(1)} %copy-done.9), kind=kOutput, calls=%fused_computation.9 | convolution fusion | flops 558891008 | bytes 7602176 | tf_op jit(solution)/shard_map/mijc,fc->mijf/dot_general | solution.py:336
  54.7 0.9 multiply_reduce_fusion
  55.6 1.4 %fusion.37 = bf16[256,512]{1,0:T(8,128)(2,1)S(1)} fusion(bf16[2,32,32,512]{3,2,1,0:T(8,128)(2,1)S(1)} %fusion.6, f32[2,32,32,256,1]{3,2,4,1,0:T(8,128)S(1)} %get-tuple-element.40, f32[256]{0:T(256)S(1)} %copy-done.11, f32[2,32,32]{2,1,0:T(8,128)S(1)} %add_rsqrt_fusion), kind=kOutput, calls=%fused_computation.51 | convolution fusion | flops 538574848 | bytes 4465664 | tf_op jit(solution)/shard_map/mijc,mijf->cf/dot_general | solution.py:340
  57.1 0.9 multiply_convert_fusion.1
  58.0 1.0 convert_bitcast_fusion
  59.0 1.8 %fusion.27 = bf16[3,256,256]{2,1,0:T(8,128)(2,1)} fusion(bf16[3,2,32,32,256]{4,3,0,1,2:T(8,128)(2,1)S(1)} %fusion.7, bf16[2,32,32,256]{3,2,1,0:T(8,128)(2,1)S(1)} %multiply_convert_fusion.1), kind=kOutput, calls=%fused_computation.47 | convolution fusion | flops 805502976 | bytes 4587520 | tf_op jit(solution)/shard_map/kmijc,mijd->kcd/dot_general | solution.py:347
  61.6 0.9 pad_maximum_fusion.2.edge_ref
  62.6 3.3 %concatenate.17 = bf16[2048,256]{1,0:T(8,128)(2,1)S(1)} concatenate(bf16[768,256]{1,0:T(8,128)(2,1)} %bitcast.177, bf16[256,256]{1,0:T(8,128)(2,1)S(1)} %get-tuple-element.20, bf16[256,256]{1,0:T(8,128)(2,1)S(1)} %get-tuple-element.19, bf16[512,256]{1,0:T(8,128)(2,1)} %fusion.34, bf16[1,256]{1,0:T(2,128)(2,1)S(1)} %convert_element_type.108, bf16[255,256]{1,0:T(8,128)(2,1)S(1)} %broadcast_in_dim.204), dimensions={0} | concatenate | bytes 2097152 | tf_op jit(solution)/shard_map/concatenate | solution.py:169
  66.0 1.1 %copy-done.1 = bf16[2,768,256]{2,1,0:T(8,128)(2,1)S(1)} copy-done((bf16[2,768,256]{2,1,0:T(8,128)(2,1)S(1)}, bf16[2,768,256]{2,1,0:T(8,128)(2,1)}, u32[]{:S(2)}) %copy-start.1) | copy-done | bytes 786456
  67.1 30.2 %sum_everywhere.1 = (bf16[32,64,256]{2,1,0:T(8,128)(2,1)S(1)}, bf16[2,768,256]{2,1,0:T(8,128)(2,1)S(1)}) custom-call(bf16[32,64,256]{2,1,0:T(8,128)(2,1)S(1)} %bitcast.171, bf16[2,768,256]{2,1,0:T(8,128)(2,1)S(1)} %copy-done.1), custom_call_target="tpu_custom_call" | custom-call | flops 30000001024 | bytes 2000000 | tf_op jit(solution)/shard_map/sum_everywhere/pallas_call | solution.py:175
  97.3 0.8 squeeze.28
  98.3 3.9 %convolution_bitcast_fusion.1 = f32[2,32,32,256]{3,2,1,0:T(8,128)S(1)} fusion(bf16[3,32,3,32,40]{4,3,0,1,2:T(8,128)(2,1)} %select_select_fusion, bf16[3,2,32,32,256]{4,3,0,2,1:T(8,128)(2,1)} %copy-done.4, bf16[3,2,32,4,256]{4,3,2,1,0:T(4,128)(2,1)S(1)} %squeeze.29, bf16[3,2,32,4,256]{4,3,2,1,0:T(4,128)(2,1)} %squeeze.28), kind=kOutput, calls=%fused_computation.35 | convolution fusion | flops 137625600 | bytes 6815744 | tf_op jit(solution)/shard_map/kijp,kmipc->mijc/dot_general | solution.py:370
  102.3 1.9 %convolution_bitcast_fusion = f32[2,32,32,256]{3,2,1,0:T(8,128)S(1)} fusion(bf16[3,32,3,32,40]{4,3,0,1,2:T(8,128)(2,1)S(1)} %copy-done.6, bf16[3,2,32,32,256]{4,3,0,2,1:T(8,128)(2,1)S(1)} %copy-done.5, bf16[3,2,32,4,256]{4,3,2,1,0:T(4,128)(2,1)S(1)} %squeeze.29, bf16[3,2,32,4,256]{4,3,2,1,0:T(4,128)(2,1)S(1)} %copy-done.8), kind=kOutput, calls=%fused_computation.34 | convolution fusion | flops 137625600 | bytes 6815744 | tf_op jit(solution)/shard_map/kijp,kmipc->mijc/dot_general | solution.py:370
  104.2 1.0 convert_multiply_fusion
  105.1 0.8 convert_multiply_fusion.1
  106.8 0.9 convert_multiply_fusion.2
  107.6 2.8 %fusion.12 = bf16[2,32,32,256]{3,2,1,0:T(8,128)(2,1)} fusion(f32[2,31,32,256]{3,2,1,0:T(8,128)S(1)} %slice.168, f32[2,31,32,256]{3,2,1,0:T(8,128)S(1)} %slice-done, bf16[2,32,32,256]{3,2,1,0:T(8,128)(2,1)S(1)} %crps_slope.1, bf16[3,32,3,32,40]{4,3,0,1,2:T(8,128)(2,1)S(1)} %copy-done.6, bf16[3,2,32,32,256]{4,3,0,2,1:T(8,128)(2,1)S(1)} %copy-done.5, ...), kind=kOutput, calls=%fused_computation.21 | convolution fusion | flops 140247040 | bytes 10878976 | tf_op jit(solution)/shard_map/kijp,kmipc->mijc/dot_general | solution.py:370
  (61 shorter events, 3.9 us)
Async XLA Ops:
  0.6 21.0 %copy-start = (bf16[3,256,256]{2,1,0:T(8,128)(2,1)S(1)}, bf16[3,256,256]{2,1,0:T(8,128)(2,1)}, u32[]{:S(2)}) copy-start(bf16[3,256,256]{2,1,0:T(8,128)(2,1)} %param.14) | copy-start | bytes 1179652
  1.8 15.7 %collective-permute-start = (bf16[2,32,4,256]{3,2,0,1:T(4,128)(2,1)S(1)}, bf16[2,32,4,256]{3,2,0,1:T(4,128)(2,1)S(1)}, u32[]{:S(2)}, u32[]{:S(2)}) collective-permute-start(bf16[2,32,4,256]{3,2,0,1:T(4,128)(2,1)S(1)} %get-tuple-element.15), channel_id=1, source_target_pairs={{0,1},{1,2},{2,3},{3,4},{4,5},{5,6},{6,7},{7,0},{8,9},{9,10},{10,1... | collective-permute-start | bytes 393224 | tf_op jit(solution)/shard_map/ppermute | solution.py:21
  2.3 15.2 %collective-permute-start.1 = (bf16[2,32,4,256]{3,2,0,1:T(4,128)(2,1)S(1)}, bf16[2,32,4,256]{3,2,0,1:T(4,128)(2,1)S(1)}, u32[]{:S(2)}, u32[]{:S(2)}) collective-permute-start(bf16[2,32,4,256]{3,2,0,1:T(4,128)(2,1)S(1)} %get-tuple-element.16), channel_id=1, source_target_pairs={{1,0},{2,1},{3,2},{4,3},{5,4},{6,5},{7,6},{0,7},{9,8},{10,9},{11,1... | collective-permute-start | bytes 393224 | tf_op jit(solution)/shard_map/ppermute | solution.py:24
  9.3 8.3 %copy-start.3 = (bf16[2,32,32,256]{3,2,1,0:T(8,128)(2,1)S(1)}, bf16[2,32,32,256]{3,2,1,0:T(8,128)(2,1)}, u32[]{:S(2)}) copy-start(bf16[2,32,32,256]{3,2,1,0:T(8,128)(2,1)} %param.9) | copy-start | bytes 3145732
  21.6 1.1 %copy-start.10 = (bf16[256,512]{1,0:T(8,128)(2,1)S(1)}, bf16[256,512]{1,0:T(8,128)(2,1)}, u32[]{:S(2)}) copy-start(bf16[256,512]{1,0:T(8,128)(2,1)} %param.15) | copy-start | bytes 786436
  21.6 1.1 %copy-start.11 = (f32[256]{0:T(256)S(1)}, f32[256]{0:T(256)}, u32[]{:S(2)}) copy-start(f32[256]{0:T(256)} %param.17) | copy-start | bytes 3076
  22.7 1.7 %copy-start.9 = (bf16[512,256]{1,0:T(8,128)(2,1)S(1)}, bf16[512,256]{1,0:T(8,128)(2,1)}, u32[]{:S(2)}) copy-start(bf16[512,256]{1,0:T(8,128)(2,1)} %param.16) | copy-start | bytes 786436
  24.4 1.0 copy-start.2
  59.0 1.8 %copy-start.4 = (bf16[3,2,32,32,256]{4,3,0,2,1:T(8,128)(2,1)}, bf16[3,2,32,32,256]{4,3,0,2,1:T(8,128)(2,1)S(1)}, u32[]{:S(2)}) copy-start(bf16[3,2,32,32,256]{4,3,0,2,1:T(8,128)(2,1)S(1)} %convert_bitcast_fusion) | copy-start | bytes 9437188
  66.0 1.1 %copy-start.1 = (bf16[2,768,256]{2,1,0:T(8,128)(2,1)S(1)}, bf16[2,768,256]{2,1,0:T(8,128)(2,1)}, u32[]{:S(2)}) copy-start(bf16[2,768,256]{2,1,0:T(8,128)(2,1)} %pad_maximum_fusion.2.edge_ref) | copy-start | bytes 2359300
  98.3 4.0 %copy-start.5 = (bf16[3,2,32,32,256]{4,3,0,2,1:T(8,128)(2,1)S(1)}, bf16[3,2,32,32,256]{4,3,0,2,1:T(8,128)(2,1)}, u32[]{:S(2)}) copy-start(bf16[3,2,32,32,256]{4,3,0,2,1:T(8,128)(2,1)} %copy-done.4) | copy-start | bytes 9437188
  98.3 4.0 %copy-start.6 = (bf16[3,32,3,32,40]{4,3,0,1,2:T(8,128)(2,1)S(1)}, bf16[3,32,3,32,40]{4,3,0,1,2:T(8,128)(2,1)}, u32[]{:S(2)}) copy-start(bf16[3,32,3,32,40]{4,3,0,1,2:T(8,128)(2,1)} %select_select_fusion) | copy-start | bytes 2211844
  98.3 4.0 %copy-start.8 = (bf16[3,2,32,4,256]{4,3,2,1,0:T(4,128)(2,1)S(1)}, bf16[3,2,32,4,256]{4,3,2,1,0:T(4,128)(2,1)}, u32[]{:S(2)}) copy-start(bf16[3,2,32,4,256]{4,3,2,1,0:T(4,128)(2,1)} %squeeze.28) | copy-start | bytes 1179652
  102.3 3.7 %copy-start.7 = (f32[2,32,32,256]{3,2,1,0:T(8,128)}, f32[2,32,32,256]{3,2,1,0:T(8,128)S(1)}, u32[]{:S(2)}) copy-start(f32[2,32,32,256]{3,2,1,0:T(8,128)S(1)} %convolution_bitcast_fusion.1) | copy-start | bytes 6291460
  106.0 1.7 %slice-start = ((f32[2,32,32,256]{3,2,1,0:T(8,128)}), f32[2,31,32,256]{3,2,1,0:T(8,128)S(1)}, s32[]{:S(2)}) async-start(f32[2,32,32,256]{3,2,1,0:T(8,128)} %copy-done.7), calls=%async_computation | async-start | bytes 4063232 | tf_op jit(solution)/shard_map/slice | solution.py:379

commit v4 on v3

--- a/solution.py
+++ b/solution.py
@@ -285,7 +285,7 @@
     devices = lax.axis_size("ens")
     here, rows, local, channels = owned.shape
     share = rows // devices
-    groups = 2 if share % 2 == 0 else 1
+    groups = next(g for g in (4, 2, 1) if share % g == 0)
     slots = (devices - 1, groups)
     whole = pl.BlockSpec(memory_space=pltpu.VMEM)
     block = slots + (here, share // groups, local, channels)

time: 111 us -> 111 us (level)
  no operation moved by 1% of the time
where the time goes in v4:
time: 111 us
  Pallas kernels  55.2 us (50%)
  matrix products  24.8 us (22%)
  other arithmetic  15.7 us (14%)
  local copies, waits for them, and re-layouts  9.13 us (8%)
  starting transfers between devices  4.61 us (4%)
    pallas_call x1, Pallas kernels, sum_everywhere(): pl.pallas_call(functools.partial(sum_kernel, members, halves), out_shape=...  30 us
    pallas_call x1, Pallas kernels, crps_slope(): pl.pallas_call(functools.partial(crps_kernel, devices, groups), out_shape...  25.2 us
    dot_general x3, matrix products, body(): jnp.einsum('kijp,kmipc->mijc', mirrored[:, :, shift_row], beside_all, pre...  8.59 us
    select_n x2, other arithmetic, band_matrix(): band = jnp.where(offset == step, taps[:, :, :, step, None, None], band)  8.27 us
    ppermute x1, starting transfers between devices, padded_2(): lax.ppermute(lax.slice_in_dim(block, 0, width, axis=dim), axis, backward)  4.1 us
    concatenate x1, local copies, waits for them, and re-layouts, sum_everywhere(): jnp.concatenate([part.astype(jnp.bfloat16) for part in parts] + [jnp.zero...  3.34 us
    dot_general x3, matrix products, body(): jnp.einsum('kijp,mipc->kmijc', ahead[:, :, shift_row], padded[:, shift_ro...  3.17 us
    dot_general x1, matrix products, body(): jnp.einsum('mijc,fc->mijf', dgrad, w_down, preferred_element_type=jnp.flo...  3.11 us
  transfers between devices with their start and end apart: 2, of which 0 were waited for; matrix products, arithmetic and copies ran while one was open for 10% of the time, Pallas kernels for 0%

profile of v4, /device:TPU:0, one launch (start us, length us, event | category | flops | bytes accessed | tf_op | source)
XLA Modules:
  0.0 110.6 jit_solution(5744282642320209051)
XLA Ops:
  0.6 1.2 %fusion.75 = (bf16[2,32,4,256]{3,2,0,1:T(4,128)(2,1)S(1)}, bf16[2,32,4,256]{3,2,0,1:T(4,128)(2,1)S(1)}) fusion(bf16[2,32,32,256]{3,2,1,0:T(8,128)(2,1)} %param.9), kind=kLoop, calls=%fused_computation.115 | loop fusion | bytes 524288 | tf_op jit(solution)/shard_map/slice | solution.py:22
  2.3 4.1 %collective-permute-start.1 = (bf16[2,32,4,256]{3,2,0,1:T(4,128)(2,1)S(1)}, bf16[2,32,4,256]{3,2,0,1:T(4,128)(2,1)S(1)}, u32[]{:S(2)}, u32[]{:S(2)}) collective-permute-start(bf16[2,32,4,256]{3,2,0,1:T(4,128)(2,1)S(1)} %get-tuple-element.16), channel_id=1, source_target_pairs={{1,0},{2,1},{3,2},{4,3},{5,4},{6,5},{7,6},{0,7},{9,8},{10,9},{11,1... | collective-permute-start | bytes 393224 | tf_op jit(solution)/shard_map/ppermute | solution.py:24
  6.5 0.8 abs_compare_fusion
  7.3 0.8 broadcast_select_fusion
  9.3 3.2 %select_select_fusion.1 = bf16[3,32,3,32,40]{4,3,0,1,2:T(8,128)(2,1)S(1)} fusion(pred[32,40]{1,0:T(8,128)(4,1)S(1)} %get-tuple-element.44, pred[32,40]{1,0:T(8,128)(4,1)S(1)} %get-tuple-element.45, pred[32,40]{1,0:T(8,128)(4,1)S(1)} %get-tuple-element.46, pred[32,40]{1,0:T(8,128)(4,1)S(1)} %get-tuple-element.47, pred[32,40]{1,0:T(8,128)(4,1)S(1)} %get-tuple-element.48, ...), kind=kLoop, calls=%fused_computation.17 | loop fusion | flops 3317760 | bytes 753984 | tf_op jit(solution)/shard_map/jit(_where)/select_n | solution.py:67
  12.5 5.0 %select_select_fusion = bf16[3,32,3,32,40]{4,3,0,1,2:T(8,128)(2,1)} fusion(pred[32,40]{1,0:T(8,128)(4,1)S(1)} %get-tuple-element.31, pred[32,40]{1,0:T(8,128)(4,1)S(1)} %get-tuple-element.32, pred[32,40]{1,0:T(8,128)(4,1)S(1)} %get-tuple-element.33, pred[32,40]{1,0:T(8,128)(4,1)S(1)} %get-tuple-element.34, pred[32,40]{1,0:T(8,128)(4,1)S(1)} %get-tuple-element.35, ...), kind=kLoop, calls=%fused_computation.16 | loop fusion | flops 3317760 | bytes 753984 | tf_op jit(solution)/shard_map/jit(_where)/select_n | solution.py:67
  17.6 0.8 pad_maximum_fusion.1
  18.4 0.9 fusion.18
  19.3 0.9 fusion.21
  20.3 1.3 %fusion.7 = bf16[3,2,32,32,256]{4,3,0,1,2:T(8,128)(2,1)S(1)} fusion(f32[32,2,256,3,32]{2,4,3,1,0:T(8,128)S(1)} %fusion.18, f32[32,2,256,3,32]{2,4,3,1,0:T(8,128)S(1)} %fusion.21, bf16[3,32,3,32,40]{4,3,0,1,2:T(8,128)(2,1)S(1)} %select_select_fusion.1, bf16[2,32,4,256]{3,2,0,1:T(4,128)(2,1)S(1)} %collective-permute-done.1, ...), kind=kOutput, calls=%fused_computation.12 | convolution fusion | flops 134479872 | bytes 17825792 | tf_op jit(solution)/shard_map/kijp,mipc->kmijc/dot_general | solution.py:317
  21.6 1.1 fusion.13
  22.7 1.6 %multiply_convert_fusion = (bf16[2,32,32,512]{3,2,1,0:T(8,128)(2,1)S(1)}, f32[2,32,32,512]{3,2,1,0:T(8,128)S(1)}) fusion(bf16[256,512]{1,0:T(8,128)(2,1)S(1)} %copy-done.10, f32[2,32,32,256,1]{3,2,4,1,0:T(8,128)S(1)} %get-tuple-element.40, f32[256]{0:T(256)S(1)} %copy-done.11, f32[2,32,32]{2,1,0:T(8,128)S(1)} %add_rsqrt_fusion), kind=kOutput, calls=%fused_computation.10 | convolution fusion | flops 547880960 | bytes 8659968 | tf_op jit(solution)/shard_map/mijc,cf->mijf/dot_general | solution.py:328
  24.4 0.7 add_convert_fusion.1.mine_ref
  25.4 25.2 %crps_slope.1 = bf16[2,32,32,256]{3,2,1,0:T(8,128)(2,1)S(1)} custom-call(bf16[2,32,32,256]{3,2,1,0:T(8,128)(2,1)S(1)} %add_convert_fusion.1.mine_ref, bf16[32,32,256]{2,1,0:T(8,128)(2,1)S(1)} %copy-done.2), custom_call_target="tpu_custom_call" | custom-call | tf_op jit(solution)/shard_map/crps_slope/pallas_call | solution.py:292
  50.6 1.5 %fusion.34 = bf16[512,256]{1,0:T(8,128)(2,1)} fusion(bf16[2,32,32,512]{3,2,1,0:T(8,128)(2,1)S(1)} %get-tuple-element.41, bf16[2,32,32,256]{3,2,1,0:T(8,128)(2,1)S(1)} %crps_slope.1), kind=kOutput, calls=%fused_computation.50 | convolution fusion | flops 537001984 | bytes 3407872 | tf_op jit(solution)/shard_map/mijf,mijc->fc/dot_general | solution.py:335
  52.1 3.1 %fusion.6 = bf16[2,32,32,512]{3,2,1,0:T(8,128)(2,1)S(1)} fusion(f32[2,32,32,512]{3,2,1,0:T(8,128)S(1)} %get-tuple-element.42, bf16[2,32,32,256]{3,2,1,0:T(8,128)(2,1)S(1)} %crps_slope.1, bf16[512,256]{1,0:T(8,128)(2,1)S(1)} %copy-done.9), kind=kOutput, calls=%fused_computation.9 | convolution fusion | flops 558891008 | bytes 7602176 | tf_op jit(solution)/shard_map/mijc,fc->mijf/dot_general | solution.py:336
  55.2 0.9 multiply_reduce_fusion
  56.1 1.4 %fusion.37 = bf16[256,512]{1,0:T(8,128)(2,1)S(1)} fusion(bf16[2,32,32,512]{3,2,1,0:T(8,128)(2,1)S(1)} %fusion.6, f32[2,32,32,256,1]{3,2,4,1,0:T(8,128)S(1)} %get-tuple-element.40, f32[256]{0:T(256)S(1)} %copy-done.11, f32[2,32,32]{2,1,0:T(8,128)S(1)} %add_rsqrt_fusion), kind=kOutput, calls=%fused_computation.51 | convolution fusion | flops 538574848 | bytes 4465664 | tf_op jit(solution)/shard_map/mijc,mijf->cf/dot_general | solution.py:340
  57.6 0.7 multiply_convert_fusion.1
  58.3 1.0 convert_bitcast_fusion
  59.4 1.8 %fusion.27 = bf16[3,256,256]{2,1,0:T(8,128)(2,1)} fusion(bf16[3,2,32,32,256]{4,3,0,1,2:T(8,128)(2,1)S(1)} %fusion.7, bf16[2,32,32,256]{3,2,1,0:T(8,128)(2,1)S(1)} %multiply_convert_fusion.1), kind=kOutput, calls=%fused_computation.47 | convolution fusion | flops 805502976 | bytes 4587520 | tf_op jit(solution)/shard_map/kmijc,mijd->kcd/dot_general | solution.py:347
  62.0 0.9 pad_maximum_fusion.2.edge_ref
  62.9 3.3 %concatenate.17 = bf16[2048,256]{1,0:T(8,128)(2,1)S(1)} concatenate(bf16[768,256]{1,0:T(8,128)(2,1)} %bitcast.177, bf16[256,256]{1,0:T(8,128)(2,1)S(1)} %get-tuple-element.20, bf16[256,256]{1,0:T(8,128)(2,1)S(1)} %get-tuple-element.19, bf16[512,256]{1,0:T(8,128)(2,1)} %fusion.34, bf16[1,256]{1,0:T(2,128)(2,1)S(1)} %convert_element_type.108, bf16[255,256]{1,0:T(8,128)(2,1)S(1)} %broadcast_in_dim.204), dimensions={0} | concatenate | bytes 2097152 | tf_op jit(solution)/shard_map/concatenate | solution.py:169
  66.3 1.1 %copy-done.1 = bf16[2,768,256]{2,1,0:T(8,128)(2,1)S(1)} copy-done((bf16[2,768,256]{2,1,0:T(8,128)(2,1)S(1)}, bf16[2,768,256]{2,1,0:T(8,128)(2,1)}, u32[]{:S(2)}) %copy-start.1) | copy-done | bytes 786456
  67.4 30.0 %sum_everywhere.1 = (bf16[32,64,256]{2,1,0:T(8,128)(2,1)S(1)}, bf16[2,768,256]{2,1,0:T(8,128)(2,1)S(1)}) custom-call(bf16[32,64,256]{2,1,0:T(8,128)(2,1)S(1)} %bitcast.171, bf16[2,768,256]{2,1,0:T(8,128)(2,1)S(1)} %copy-done.1), custom_call_target="tpu_custom_call" | custom-call | flops 30000001024 | bytes 2000000 | tf_op jit(solution)/shard_map/sum_everywhere/pallas_call | solution.py:175
  97.5 0.8 squeeze.28
  98.5 3.9 %convolution_bitcast_fusion.1 = f32[2,32,32,256]{3,2,1,0:T(8,128)S(1)} fusion(bf16[3,32,3,32,40]{4,3,0,1,2:T(8,128)(2,1)} %select_select_fusion, bf16[3,2,32,32,256]{4,3,0,2,1:T(8,128)(2,1)} %copy-done.4, bf16[3,2,32,4,256]{4,3,2,1,0:T(4,128)(2,1)S(1)} %squeeze.29, bf16[3,2,32,4,256]{4,3,2,1,0:T(4,128)(2,1)} %squeeze.28), kind=kOutput, calls=%fused_computation.35 | convolution fusion | flops 137625600 | bytes 6815744 | tf_op jit(solution)/shard_map/kijp,kmipc->mijc/dot_general | solution.py:370
  102.5 1.9 %convolution_bitcast_fusion = f32[2,32,32,256]{3,2,1,0:T(8,128)S(1)} fusion(bf16[3,32,3,32,40]{4,3,0,1,2:T(8,128)(2,1)S(1)} %copy-done.6, bf16[3,2,32,32,256]{4,3,0,2,1:T(8,128)(2,1)S(1)} %copy-done.5, bf16[3,2,32,4,256]{4,3,2,1,0:T(4,128)(2,1)S(1)} %squeeze.29, bf16[3,2,32,4,256]{4,3,2,1,0:T(4,128)(2,1)S(1)} %copy-done.8), kind=kOutput, calls=%fused_computation.34 | convolution fusion | flops 137625600 | bytes 6815744 | tf_op jit(solution)/shard_map/kijp,kmipc->mijc/dot_general | solution.py:370
  104.3 1.0 convert_multiply_fusion
  105.3 0.8 convert_multiply_fusion.1
  107.0 0.9 convert_multiply_fusion.2
  107.8 2.8 %fusion.12 = bf16[2,32,32,256]{3,2,1,0:T(8,128)(2,1)} fusion(f32[2,31,32,256]{3,2,1,0:T(8,128)S(1)} %slice.168, f32[2,31,32,256]{3,2,1,0:T(8,128)S(1)} %slice-done, bf16[2,32,32,256]{3,2,1,0:T(8,128)(2,1)S(1)} %crps_slope.1, bf16[3,32,3,32,40]{4,3,0,1,2:T(8,128)(2,1)S(1)} %copy-done.6, bf16[3,2,32,32,256]{4,3,0,2,1:T(8,128)(2,1)S(1)} %copy-done.5, ...), kind=kOutput, calls=%fused_computation.21 | convolution fusion | flops 140247040 | bytes 10878976 | tf_op jit(solution)/shard_map/kijp,kmipc->mijc/dot_general | solution.py:370
  (61 shorter events, 3.9 us)
Async XLA Ops:
  0.6 21.0 %copy-start = (bf16[3,256,256]{2,1,0:T(8,128)(2,1)S(1)}, bf16[3,256,256]{2,1,0:T(8,128)(2,1)}, u32[]{:S(2)}) copy-start(bf16[3,256,256]{2,1,0:T(8,128)(2,1)} %param.14) | copy-start | bytes 1179652
  1.8 15.7 %collective-permute-start = (bf16[2,32,4,256]{3,2,0,1:T(4,128)(2,1)S(1)}, bf16[2,32,4,256]{3,2,0,1:T(4,128)(2,1)S(1)}, u32[]{:S(2)}, u32[]{:S(2)}) collective-permute-start(bf16[2,32,4,256]{3,2,0,1:T(4,128)(2,1)S(1)} %get-tuple-element.15), channel_id=1, source_target_pairs={{0,1},{1,2},{2,3},{3,4},{4,5},{5,6},{6,7},{7,0},{8,9},{9,10},{10,1... | collective-permute-start | bytes 393224 | tf_op jit(solution)/shard_map/ppermute | solution.py:21
  2.3 15.2 %collective-permute-start.1 = (bf16[2,32,4,256]{3,2,0,1:T(4,128)(2,1)S(1)}, bf16[2,32,4,256]{3,2,0,1:T(4,128)(2,1)S(1)}, u32[]{:S(2)}, u32[]{:S(2)}) collective-permute-start(bf16[2,32,4,256]{3,2,0,1:T(4,128)(2,1)S(1)} %get-tuple-element.16), channel_id=1, source_target_pairs={{1,0},{2,1},{3,2},{4,3},{5,4},{6,5},{7,6},{0,7},{9,8},{10,9},{11,1... | collective-permute-start | bytes 393224 | tf_op jit(solution)/shard_map/ppermute | solution.py:24
  9.3 8.3 %copy-start.3 = (bf16[2,32,32,256]{3,2,1,0:T(8,128)(2,1)S(1)}, bf16[2,32,32,256]{3,2,1,0:T(8,128)(2,1)}, u32[]{:S(2)}) copy-start(bf16[2,32,32,256]{3,2,1,0:T(8,128)(2,1)} %param.9) | copy-start | bytes 3145732
  21.6 1.1 %copy-start.10 = (bf16[256,512]{1,0:T(8,128)(2,1)S(1)}, bf16[256,512]{1,0:T(8,128)(2,1)}, u32[]{:S(2)}) copy-start(bf16[256,512]{1,0:T(8,128)(2,1)} %param.15) | copy-start | bytes 786436
  21.6 1.1 %copy-start.11 = (f32[256]{0:T(256)S(1)}, f32[256]{0:T(256)}, u32[]{:S(2)}) copy-start(f32[256]{0:T(256)} %param.17) | copy-start | bytes 3076
  22.7 1.7 %copy-start.9 = (bf16[512,256]{1,0:T(8,128)(2,1)S(1)}, bf16[512,256]{1,0:T(8,128)(2,1)}, u32[]{:S(2)}) copy-start(bf16[512,256]{1,0:T(8,128)(2,1)} %param.16) | copy-start | bytes 786436
  24.4 1.0 copy-start.2
  59.4 1.8 %copy-start.4 = (bf16[3,2,32,32,256]{4,3,0,2,1:T(8,128)(2,1)}, bf16[3,2,32,32,256]{4,3,0,2,1:T(8,128)(2,1)S(1)}, u32[]{:S(2)}) copy-start(bf16[3,2,32,32,256]{4,3,0,2,1:T(8,128)(2,1)S(1)} %convert_bitcast_fusion) | copy-start | bytes 9437188
  66.3 1.1 %copy-start.1 = (bf16[2,768,256]{2,1,0:T(8,128)(2,1)S(1)}, bf16[2,768,256]{2,1,0:T(8,128)(2,1)}, u32[]{:S(2)}) copy-start(bf16[2,768,256]{2,1,0:T(8,128)(2,1)} %pad_maximum_fusion.2.edge_ref) | copy-start | bytes 2359300
  98.5 4.0 %copy-start.5 = (bf16[3,2,32,32,256]{4,3,0,2,1:T(8,128)(2,1)S(1)}, bf16[3,2,32,32,256]{4,3,0,2,1:T(8,128)(2,1)}, u32[]{:S(2)}) copy-start(bf16[3,2,32,32,256]{4,3,0,2,1:T(8,128)(2,1)} %copy-done.4) | copy-start | bytes 9437188
  98.5 4.0 %copy-start.6 = (bf16[3,32,3,32,40]{4,3,0,1,2:T(8,128)(2,1)S(1)}, bf16[3,32,3,32,40]{4,3,0,1,2:T(8,128)(2,1)}, u32[]{:S(2)}) copy-start(bf16[3,32,3,32,40]{4,3,0,1,2:T(8,128)(2,1)} %select_select_fusion) | copy-start | bytes 2211844
  98.5 4.0 %copy-start.8 = (bf16[3,2,32,4,256]{4,3,2,1,0:T(4,128)(2,1)S(1)}, bf16[3,2,32,4,256]{4,3,2,1,0:T(4,128)(2,1)}, u32[]{:S(2)}) copy-start(bf16[3,2,32,4,256]{4,3,2,1,0:T(4,128)(2,1)} %squeeze.28) | copy-start | bytes 1179652
  102.4 3.7 %copy-start.7 = (f32[2,32,32,256]{3,2,1,0:T(8,128)}, f32[2,32,32,256]{3,2,1,0:T(8,128)S(1)}, u32[]{:S(2)}) copy-start(f32[2,32,32,256]{3,2,1,0:T(8,128)S(1)} %convolution_bitcast_fusion.1) | copy-start | bytes 6291460
  106.1 1.7 %slice-start = ((f32[2,32,32,256]{3,2,1,0:T(8,128)}), f32[2,31,32,256]{3,2,1,0:T(8,128)S(1)}, s32[]{:S(2)}) async-start(f32[2,32,32,256]{3,2,1,0:T(8,128)} %copy-done.7), calls=%async_computation | async-start | bytes 4063232 | tf_op jit(solution)/shard_map/slice | solution.py:379

commit v5 on v3

--- a/solution.py
+++ b/solution.py
@@ -62,10 +62,11 @@
         offset = 2 * reach + along - across
     else:
         offset = across - along
-    band = jnp.zeros(taps.shape[:3] + offset.shape, taps.dtype)
-    for step in range(count):
-        band = jnp.where(offset == step, taps[:, :, :, step, None, None], band)
-    return band
+    steps = jnp.arange(count, dtype=jnp.int32)[:, None, None]
+    picks = (offset[None] == steps).astype(taps.dtype)
+    return jnp.einsum("kiat,tjp->kiajp", taps, picks, preferred_element_type=jnp.float32).astype(
+        taps.dtype
+    )
 
 
 def sum_kernel(members, halves, part_ref, edge_ref, full_ref, beside_ref, sum_core, sum_ens, from_core, from_ens, from_space, send, recv):

time: 111 us -> 108 us (0.973)
  other arithmetic: 15.9 us -> 7.36 us
  matrix products: 24.7 us -> 27.4 us
  local copies, waits for them, and re-layouts: 9.13 us -> 11.6 us
    select_n x2 -> x0, other arithmetic: 8.27 us -> none  [band_matrix(): band = jnp.where(offset == step, taps[:, :, :, step, None, None], band)]
    unnamed x24, local copies, waits for them, and re-layouts: 1.5 us -> 3.65 us
    squeeze x0 -> x2, local copies, waits for them, and re-layouts: none -> 1.88 us  [the longest x1 1.47 us: body(): mirrored[:, :, shift_row]]
    dot_general x0 -> x2, matrix products: none -> 1.59 us  [band_matrix(): jnp.einsum('kiat,tjp->kiajp', taps, picks, preferred_element_type=jnp.flo...]
  transfers between devices with their start and end apart: 2 -> 2, of which waited for: 0 -> 0; matrix products, arithmetic and copies ran while one was open for 10% -> 5% of each run, Pallas kernels for 0% -> 0%
where the time goes in v5:
time: 108 us; the launch traced here: 107 us
  Pallas kernels  55.2 us (51%)
  matrix products  27.4 us (25%)
  local copies, waits for them, and re-layouts  11.6 us (11%)
  other arithmetic  7.36 us (7%)
  starting transfers between devices  4.61 us (4%)
    pallas_call x1, Pallas kernels, sum_everywhere(): pl.pallas_call(functools.partial(sum_kernel, members, halves), out_shape=...  30 us
    pallas_call x1, Pallas kernels, crps_slope(): pl.pallas_call(functools.partial(crps_kernel, devices, groups), out_shape...  25.2 us
    dot_general x3, matrix products, body(): jnp.einsum('kijp,kmipc->mijc', mirrored[:, :, shift_row], beside_all, pre...  8.93 us
    ppermute x1, starting transfers between devices, padded_2(): lax.ppermute(lax.slice_in_dim(block, 0, width, axis=dim), axis, backward)  4.1 us
    dot_general x3, matrix products, body(): jnp.einsum('kijp,mipc->kmijc', ahead[:, :, shift_row], padded[:, shift_ro...  3.91 us
    unnamed x24, local copies, waits for them, and re-layouts  3.65 us
    concatenate x1, local copies, waits for them, and re-layouts, sum_everywhere(): jnp.concatenate([part.astype(jnp.bfloat16) for part in parts] + [jnp.zero...  3.34 us
    dot_general x1, matrix products, body(): jnp.einsum('mijc,fc->mijf', dgrad, w_down, preferred_element_type=jnp.flo...  2.94 us
  transfers between devices with their start and end apart: 2, of which 0 were waited for; matrix products, arithmetic and copies ran while one was open for 5% of the time, Pallas kernels for 0%

profile of v5, /device:TPU:0, one launch (start us, length us, event | category | flops | bytes accessed | tf_op | source)
XLA Modules:
  0.0 107.1 jit_solution(11821497953258638993)
XLA Ops:
  0.6 1.2 %fusion.74 = (bf16[2,32,4,256]{3,2,0,1:T(4,128)(2,1)S(1)}, bf16[2,32,4,256]{3,2,0,1:T(4,128)(2,1)S(1)}) fusion(bf16[2,32,32,256]{3,2,1,0:T(8,128)(2,1)} %param.9), kind=kLoop, calls=%fused_computation.105 | loop fusion | bytes 524288 | tf_op jit(solution)/shard_map/slice | solution.py:22
  2.3 4.1 %collective-permute-start.1 = (bf16[2,32,4,256]{3,2,0,1:T(4,128)(2,1)S(1)}, bf16[2,32,4,256]{3,2,0,1:T(4,128)(2,1)S(1)}, u32[]{:S(2)}, u32[]{:S(2)}) collective-permute-start(bf16[2,32,4,256]{3,2,0,1:T(4,128)(2,1)S(1)} %get-tuple-element.22), channel_id=1, source_target_pairs={{1,0},{2,1},{3,2},{4,3},{5,4},{6,5},{7,6},{0,7},{9,8},{10,9},{11,1... | collective-permute-start | bytes 393224 | tf_op jit(solution)/shard_map/ppermute | solution.py:24
  6.5 0.7 abs_compare_fusion
  7.2 0.8 select_bitcast_fusion
  8.0 0.8 convolution_convert_fusion.1
  9.3 0.8 convolution_convert_fusion
  10.1 1.5 %slice_bitcast_fusion.2 = (bf16[3,32,32,40]{3,1,2,0:T(8,128)(2,1)}, bf16[3,32,32,40]{3,1,2,0:T(8,128)(2,1)}, bf16[3,32,32,40]{3,1,2,0:T(8,128)(2,1)}) fusion(bf16[3,32,3,32,40]{4,1,3,2,0:T(8,128)(2,1)S(1)} %convolution_convert_fusion), kind=kLoop, calls=%fused_computation.58 | loop fusion | bytes 1474560 | tf_op jit(solution)/shard_map/squeeze | solution.py:373
  11.9 0.8 pad_maximum_fusion.1
  12.7 0.9 fusion.18
  13.7 0.9 fusion.21
  14.6 2.0 %fusion.7 = bf16[3,2,32,32,256]{4,3,0,1,2:T(8,128)(2,1)S(1)} fusion(f32[32,2,256,3,32]{2,4,3,1,0:T(8,128)S(1)} %fusion.18, f32[32,2,256,3,32]{2,4,3,1,0:T(8,128)S(1)} %fusion.21, bf16[3,32,32,40,1]{3,1,2,0,4:T(8,128)(2,1)S(1)} %get-tuple-element.16, bf16[2,32,4,256]{3,2,0,1:T(4,128)(2,1)S(1)} %collective-permute-done.1, ...), kind=kOutput, calls=%fused_computation.12 | convolution fusion | flops 134479872 | bytes 17285120 | tf_op jit(solution)/shard_map/kijp,mipc->kmijc/dot_general | solution.py:318
  16.7 1.1 fusion.13
  17.8 1.7 %multiply_convert_fusion = (bf16[2,32,32,512]{3,2,1,0:T(8,128)(2,1)S(1)}, f32[2,32,32,512]{3,2,1,0:T(8,128)S(1)}) fusion(bf16[256,512]{1,0:T(8,128)(2,1)S(1)} %copy-done.10, f32[2,32,32,256,1]{3,2,4,1,0:T(8,128)S(1)} %get-tuple-element.28, f32[256]{0:T(256)S(1)} %copy-done.11, f32[2,32,32]{2,1,0:T(8,128)S(1)} %add_rsqrt_fusion), kind=kOutput, calls=%fused_computation.10 | convolution fusion | flops 547880960 | bytes 8659968 | tf_op jit(solution)/shard_map/mijc,cf->mijf/dot_general | solution.py:329
  20.5 25.2 %crps_slope.1 = bf16[2,32,32,256]{3,2,1,0:T(8,128)(2,1)S(1)} custom-call(bf16[2,32,32,256]{3,2,1,0:T(8,128)(2,1)S(1)} %add_convert_fusion.1.mine_ref, bf16[32,32,256]{2,1,0:T(8,128)(2,1)S(1)} %copy-done.3), custom_call_target="tpu_custom_call" | custom-call | tf_op jit(solution)/shard_map/crps_slope/pallas_call | solution.py:293
  45.7 1.5 %fusion.34 = bf16[512,256]{1,0:T(8,128)(2,1)} fusion(bf16[2,32,32,512]{3,2,1,0:T(8,128)(2,1)S(1)} %get-tuple-element.29, bf16[2,32,32,256]{3,2,1,0:T(8,128)(2,1)S(1)} %crps_slope.1), kind=kOutput, calls=%fused_computation.50 | convolution fusion | flops 537001984 | bytes 3407872 | tf_op jit(solution)/shard_map/mijf,mijc->fc/dot_general | solution.py:336
  47.2 2.9 %fusion.6 = bf16[2,32,32,512]{3,2,1,0:T(8,128)(2,1)S(1)} fusion(f32[2,32,32,512]{3,2,1,0:T(8,128)S(1)} %get-tuple-element.30, bf16[2,32,32,256]{3,2,1,0:T(8,128)(2,1)S(1)} %crps_slope.1, bf16[512,256]{1,0:T(8,128)(2,1)S(1)} %copy-done.9), kind=kOutput, calls=%fused_computation.9 | convolution fusion | flops 558891008 | bytes 7602176 | tf_op jit(solution)/shard_map/mijc,fc->mijf/dot_general | solution.py:337
  50.1 0.9 multiply_reduce_fusion
  51.0 1.4 %fusion.37 = bf16[256,512]{1,0:T(8,128)(2,1)S(1)} fusion(bf16[2,32,32,512]{3,2,1,0:T(8,128)(2,1)S(1)} %fusion.6, f32[2,32,32,256,1]{3,2,4,1,0:T(8,128)S(1)} %get-tuple-element.28, f32[256]{0:T(256)S(1)} %copy-done.11, f32[2,32,32]{2,1,0:T(8,128)S(1)} %add_rsqrt_fusion), kind=kOutput, calls=%fused_computation.51 | convolution fusion | flops 538574848 | bytes 4465664 | tf_op jit(solution)/shard_map/mijc,mijf->cf/dot_general | solution.py:341
  52.5 0.7 multiply_convert_fusion.1
  53.2 1.0 convert_bitcast_fusion
  54.3 1.8 %fusion.27 = bf16[3,256,256]{2,1,0:T(8,128)(2,1)} fusion(bf16[3,2,32,32,256]{4,3,0,1,2:T(8,128)(2,1)S(1)} %fusion.7, bf16[2,32,32,256]{3,2,1,0:T(8,128)(2,1)S(1)} %multiply_convert_fusion.1), kind=kOutput, calls=%fused_computation.47 | convolution fusion | flops 805502976 | bytes 4587520 | tf_op jit(solution)/shard_map/kmijc,mijd->kcd/dot_general | solution.py:348
  56.9 0.9 pad_maximum_fusion.2.edge_ref
  57.8 3.3 %concatenate.17 = bf16[2048,256]{1,0:T(8,128)(2,1)S(1)} concatenate(bf16[768,256]{1,0:T(8,128)(2,1)} %bitcast.169, bf16[256,256]{1,0:T(8,128)(2,1)S(1)} %get-tuple-element.26, bf16[256,256]{1,0:T(8,128)(2,1)S(1)} %get-tuple-element.25, bf16[512,256]{1,0:T(8,128)(2,1)} %fusion.34, bf16[1,256]{1,0:T(2,128)(2,1)S(1)} %convert_element_type.117, bf16[255,256]{1,0:T(8,128)(2,1)S(1)} %broadcast_in_dim.14), dimensions={0} | concatenate | bytes 2097152 | tf_op jit(solution)/shard_map/concatenate | solution.py:170
  61.2 1.1 %copy-done.2 = bf16[2,768,256]{2,1,0:T(8,128)(2,1)S(1)} copy-done((bf16[2,768,256]{2,1,0:T(8,128)(2,1)S(1)}, bf16[2,768,256]{2,1,0:T(8,128)(2,1)}, u32[]{:S(2)}) %copy-start.2) | copy-done | bytes 786456
  62.3 30.0 %sum_everywhere.1 = (bf16[32,64,256]{2,1,0:T(8,128)(2,1)S(1)}, bf16[2,768,256]{2,1,0:T(8,128)(2,1)S(1)}) custom-call(bf16[32,64,256]{2,1,0:T(8,128)(2,1)S(1)} %bitcast.163, bf16[2,768,256]{2,1,0:T(8,128)(2,1)S(1)} %copy-done.2), custom_call_target="tpu_custom_call" | custom-call | flops 30000001024 | bytes 2000000 | tf_op jit(solution)/shard_map/sum_everywhere/pallas_call | solution.py:176
  92.3 1.0 convert_multiply_fusion
  93.3 0.8 convert_multiply_fusion.1
  94.4 3.8 %convolution_bitcast_fusion.1 = f32[2,32,32,256]{3,2,1,0:T(8,128)S(1)} fusion(bf16[3,32,32,40]{3,1,2,0:T(8,128)(2,1)} %get-tuple-element.15, bf16[3,2,32,32,256]{4,3,0,2,1:T(8,128)(2,1)} %copy-done.5, bf16[3,2,32,4,256]{4,3,2,1,0:T(4,128)(2,1)S(1)} %squeeze.29, bf16[3,2,32,4,256]{4,3,2,1,0:T(4,128)(2,1)S(1)} %squeeze.28), kind=kOutput, calls=%fused_computation.35 | convolution fusion | flops 137625600 | bytes 6275072 | tf_op jit(solution)/shard_map/kijp,kmipc->mijc/dot_general | solution.py:371
  98.4 1.6 %copy-done.6 = bf16[3,2,32,32,256]{4,3,0,2,1:T(8,128)(2,1)S(1)} copy-done((bf16[3,2,32,32,256]{4,3,0,2,1:T(8,128)(2,1)S(1)}, bf16[3,2,32,32,256]{4,3,0,2,1:T(8,128)(2,1)}, u32[]{:S(2)}) %copy-start.6) | copy-done | bytes 3145752
  100.2 2.1 %convolution_bitcast_fusion = f32[2,32,32,256]{3,2,1,0:T(8,128)S(1)} fusion(bf16[3,32,32,40]{3,1,2,0:T(8,128)(2,1)S(1)} %copy-done.8, bf16[3,2,32,32,256]{4,3,0,2,1:T(8,128)(2,1)S(1)} %copy-done.6, bf16[3,2,32,4,256]{4,3,2,1,0:T(4,128)(2,1)S(1)} %squeeze.29, bf16[3,2,32,4,256]{4,3,2,1,0:T(4,128)(2,1)S(1)} %squeeze.28), kind=kOutput, calls=%fused_computation.34 | convolution fusion | flops 137625600 | bytes 6275072 | tf_op jit(solution)/shard_map/kijp,kmipc->mijc/dot_general | solution.py:371
  103.1 0.9 convert_multiply_fusion.2
  104.0 3.1 %fusion.12 = bf16[2,32,32,256]{3,2,1,0:T(8,128)(2,1)} fusion(f32[2,31,32,256]{3,2,1,0:T(8,128)S(1)} %slice.114, f32[2,31,32,256]{3,2,1,0:T(8,128)S(1)} %slice.112, bf16[2,32,32,256]{3,2,1,0:T(8,128)(2,1)S(1)} %crps_slope.1, bf16[3,32,32,40]{3,1,2,0:T(8,128)(2,1)S(1)} %copy-done.7, bf16[3,2,32,32,256]{4,3,0,2,1:T(8,128)(2,1)S(1)} %copy-done.6, ...), kind=kOutput, calls=%fused_computation.19 | convolution fusion | flops 140247040 | bytes 10338304 | tf_op jit(solution)/shard_map/kijp,kmipc->mijc/dot_general | solution.py:371
  (48 shorter events, 4.7 us)
Async XLA Ops:
  0.6 16.0 %copy-start = (bf16[3,256,256]{2,1,0:T(8,128)(2,1)S(1)}, bf16[3,256,256]{2,1,0:T(8,128)(2,1)}, u32[]{:S(2)}) copy-start(bf16[3,256,256]{2,1,0:T(8,128)(2,1)} %param.14) | copy-start | bytes 1179652
  1.8 9.7 %collective-permute-start = (bf16[2,32,4,256]{3,2,0,1:T(4,128)(2,1)S(1)}, bf16[2,32,4,256]{3,2,0,1:T(4,128)(2,1)S(1)}, u32[]{:S(2)}, u32[]{:S(2)}) collective-permute-start(bf16[2,32,4,256]{3,2,0,1:T(4,128)(2,1)S(1)} %get-tuple-element.21), channel_id=1, source_target_pairs={{0,1},{1,2},{2,3},{3,4},{4,5},{5,6},{6,7},{7,0},{8,9},{9,10},{10,1... | collective-permute-start | bytes 393224 | tf_op jit(solution)/shard_map/ppermute | solution.py:21
  2.3 9.2 %collective-permute-start.1 = (bf16[2,32,4,256]{3,2,0,1:T(4,128)(2,1)S(1)}, bf16[2,32,4,256]{3,2,0,1:T(4,128)(2,1)S(1)}, u32[]{:S(2)}, u32[]{:S(2)}) collective-permute-start(bf16[2,32,4,256]{3,2,0,1:T(4,128)(2,1)S(1)} %get-tuple-element.22), channel_id=1, source_target_pairs={{1,0},{2,1},{3,2},{4,3},{5,4},{6,5},{7,6},{0,7},{9,8},{10,9},{11,1... | collective-permute-start | bytes 393224 | tf_op jit(solution)/shard_map/ppermute | solution.py:24
  10.1 1.8 %copy-start.4 = (bf16[2,32,32,256]{3,2,1,0:T(8,128)(2,1)S(1)}, bf16[2,32,32,256]{3,2,1,0:T(8,128)(2,1)}, u32[]{:S(2)}) copy-start(bf16[2,32,32,256]{3,2,1,0:T(8,128)(2,1)} %param.9) | copy-start | bytes 3145732
  16.7 1.1 %copy-start.10 = (bf16[256,512]{1,0:T(8,128)(2,1)S(1)}, bf16[256,512]{1,0:T(8,128)(2,1)}, u32[]{:S(2)}) copy-start(bf16[256,512]{1,0:T(8,128)(2,1)} %param.15) | copy-start | bytes 786436
  16.7 1.1 %copy-start.11 = (f32[256]{0:T(256)S(1)}, f32[256]{0:T(256)}, u32[]{:S(2)}) copy-start(f32[256]{0:T(256)} %param.17) | copy-start | bytes 3076
  17.8 1.7 %copy-start.9 = (bf16[512,256]{1,0:T(8,128)(2,1)S(1)}, bf16[512,256]{1,0:T(8,128)(2,1)}, u32[]{:S(2)}) copy-start(bf16[512,256]{1,0:T(8,128)(2,1)} %param.16) | copy-start | bytes 786436
  19.5 1.0 copy-start.3
  54.3 1.8 %copy-start.5 = (bf16[3,2,32,32,256]{4,3,0,2,1:T(8,128)(2,1)}, bf16[3,2,32,32,256]{4,3,0,2,1:T(8,128)(2,1)S(1)}, u32[]{:S(2)}) copy-start(bf16[3,2,32,32,256]{4,3,0,2,1:T(8,128)(2,1)S(1)} %convert_bitcast_fusion) | copy-start | bytes 9437188
  61.2 1.1 %copy-start.2 = (bf16[2,768,256]{2,1,0:T(8,128)(2,1)S(1)}, bf16[2,768,256]{2,1,0:T(8,128)(2,1)}, u32[]{:S(2)}) copy-start(bf16[2,768,256]{2,1,0:T(8,128)(2,1)} %pad_maximum_fusion.2.edge_ref) | copy-start | bytes 2359300
  98.1 1.9 %copy-start.6 = (bf16[3,2,32,32,256]{4,3,0,2,1:T(8,128)(2,1)S(1)}, bf16[3,2,32,32,256]{4,3,0,2,1:T(8,128)(2,1)}, u32[]{:S(2)}) copy-start(bf16[3,2,32,32,256]{4,3,0,2,1:T(8,128)(2,1)} %copy-done.5) | copy-start | bytes 9437188
  98.2 2.1 %copy-start.8 = (bf16[3,32,32,40]{3,1,2,0:T(8,128)(2,1)S(1)}, bf16[3,32,32,40]{3,1,2,0:T(8,128)(2,1)}, u32[]{:S(2)}) copy-start(bf16[3,32,32,40]{3,1,2,0:T(8,128)(2,1)} %get-tuple-element.14) | copy-start | bytes 737284
  102.3 1.7 %copy-start.7 = (bf16[3,32,32,40]{3,1,2,0:T(8,128)(2,1)S(1)}, bf16[3,32,32,40]{3,1,2,0:T(8,128)(2,1)}, u32[]{:S(2)}) copy-start(bf16[3,32,32,40]{3,1,2,0:T(8,128)(2,1)} %get-tuple-element.13) | copy-start | bytes 737284
  104.0 3.1 %copy-start.1 = (bf16[3,256,256]{2,1,0:T(8,128)(2,1)S(1)}, bf16[3,256,256]{2,1,0:T(8,128)(2,1)}, u32[]{:S(2)}) copy-start(bf16[3,256,256]{2,1,0:T(8,128)(2,1)} %param.14) | copy-start | bytes 1179652
